TPU v7x, 32 devices: a whole 2x2x4 slice. The times are simulated.
32 devices in a mesh: ctx: 8 (over z, x), tp: 4 (over y, core).
Axes of the slice: x: 2, y: 2, z: 4, core: 2. Of those that a mesh axis runs over, the one named last changes fastest.
Arguments:
- tokens: bfloat16 [4, 512, 2048], P(None, 'ctx'), may hold values from -6 to 6
- cotangent: bfloat16 [4, 512, 2048], P(None, 'ctx'), may hold values from -6 to 6
- routes: int32 [4, 512, 8], P(None, 'ctx'), may hold values from 0 to 15, all different within a row; in each aligned block of 64 rows (0 to 63, 64 to 127, ..., all dimensions but the last counted through in order) at most 48 rows name the same one
- attn_gain: bfloat16 [2048], P('ctx'), may hold values from 0.099609375 to 1.8984375
- ffn_gain: bfloat16 [2048], P('ctx'), may hold values from 0.099609375 to 1.8984375
- qk_gain: bfloat16 [128, 2], P('ctx'), may hold values from 0.099609375 to 1.8984375
- w_query: bfloat16 [2048, 2048], P('ctx', 'tp'), may hold values from -0.125 to 0.125
- w_key: bfloat16 [2048, 2048], P('ctx', 'tp'), may hold values from -0.125 to 0.125
- w_value: bfloat16 [2048, 2048], P('ctx', 'tp'), may hold values from -0.125 to 0.125
- w_out: bfloat16 [2048, 2048], P('ctx', 'tp'), may hold values from -1.5 to 1.5
- router: bfloat16 [2048, 16], P('ctx'), may hold values from -0.0625 to 0.0625
- w_gate: bfloat16 [16, 2048, 1024], P(None, 'ctx', 'tp'), may hold values from -0.125 to 0.125
- w_up: bfloat16 [16, 2048, 1024], P(None, 'ctx', 'tp'), may hold values from -0.125 to 0.125
- w_down: bfloat16 [16, 2048, 1024], P(None, 'ctx', 'tp'), may hold values from -1.5 to 1.5
Outputs:
- layer_out: bfloat16 [4, 512, 2048], P(None, 'ctx')
- input_grad: bfloat16 [4, 512, 2048], P(None, 'ctx')
- grad_attn_gain: float32 [2048], P('ctx')
- grad_ffn_gain: float32 [2048], P('ctx')
- grad_qk_gain: float32 [128, 2], P('ctx')
- grad_query: float32 [2048, 2048], P('ctx', 'tp')
- grad_key: float32 [2048, 2048], P('ctx', 'tp')
- grad_value: float32 [2048, 2048], P('ctx', 'tp')
- grad_out: float32 [2048, 2048], P('ctx', 'tp')
- grad_router: float32 [2048, 16], P('ctx')
- grad_gate: float32 [16, 2048, 1024], P(None, 'ctx', 'tp')
- grad_up: float32 [16, 2048, 1024], P(None, 'ctx', 'tp')
- grad_down: float32 [16, 2048, 1024], P(None, 'ctx', 'tp')
Inputs may be any that keep to these rules, and one draw needn't show every extreme that they name: `routes`: A token names 8 different experts. Among the 64 tokens of one sequence that one device holds, no expert is named more than 48 times, and in some such block one expert is named exactly 48 times.
All inputs are finite; a program needn't handle non-finite values.
Results may differ from a plain program's by a relative error of at most 0.024.
Values may be sent and summed in bfloat16 or wider, within the bound.
A program may use at most 320 MiB of HBM per device.

v0:
```python
import jax
import jax.numpy as jnp
from jax import lax
from jax.sharding import PartitionSpec as P

MICRO = 2
MOST = 48


EPS = 1e-06
ROPE_BASE = 50000.0


def product(left_op, right_op):
    return jnp.dot(left_op, right_op, preferred_element_type=jnp.float32)


def rotate(values, cosines, sines):
    half_size = values.shape[-1] // 2
    first_half = values[..., :half_size]
    second_half = values[..., half_size:]
    return jnp.concatenate(
        [first_half * cosines - second_half * sines, second_half * cosines + first_half * sines],
        axis=-1,
    )


def inverse_rms(values):
    return lax.rsqrt(jnp.mean(values * values, axis=-1, keepdims=True) + EPS)


def norm_back(gradient, inputs, scaling, gain_vec):
    weighted = gradient * gain_vec
    return scaling * weighted - inputs * scaling**3 * jnp.mean(
        weighted * inputs, axis=-1, keepdims=True
    )


def fetch_dense(attn_gain, ffn_gain, qk_gain, w_query, w_key, w_value, w_out, router):
    return (
        lax.all_gather(attn_gain, "ctx", axis=0, tiled=True),
        lax.all_gather(ffn_gain, "ctx", axis=0, tiled=True),
        lax.all_gather(qk_gain, "ctx", axis=0, tiled=True),
        lax.all_gather(w_query, "ctx", axis=0, tiled=True),
        lax.all_gather(w_key, "ctx", axis=0, tiled=True),
        lax.all_gather(w_value, "ctx", axis=0, tiled=True),
        lax.all_gather(w_out, "ctx", axis=0, tiled=True),
        lax.all_gather(router, "ctx", axis=0, tiled=True),
    )


def fetch_experts(w_gate, w_up, w_down):
    return (
        lax.all_gather(w_gate, "ctx", axis=1, tiled=True),
        lax.all_gather(w_up, "ctx", axis=1, tiled=True),
        lax.all_gather(w_down, "ctx", axis=1, tiled=True),
    )


def reduce_grads(dense_grads, expert_grads):
    dense_owned = (
        lax.psum_scatter(
            dense_grads[0].astype(jnp.bfloat16), "ctx", scatter_dimension=0, tiled=True
        ).astype(jnp.float32),
        lax.psum_scatter(
            dense_grads[1].astype(jnp.bfloat16), "ctx", scatter_dimension=0, tiled=True
        ).astype(jnp.float32),
        lax.psum_scatter(
            dense_grads[2].astype(jnp.bfloat16), "ctx", scatter_dimension=0, tiled=True
        ).astype(jnp.float32),
        lax.psum_scatter(
            dense_grads[3].astype(jnp.bfloat16), "ctx", scatter_dimension=0, tiled=True
        ).astype(jnp.float32),
        lax.psum_scatter(
            dense_grads[4].astype(jnp.bfloat16), "ctx", scatter_dimension=0, tiled=True
        ).astype(jnp.float32),
        lax.psum_scatter(
            dense_grads[5].astype(jnp.bfloat16), "ctx", scatter_dimension=0, tiled=True
        ).astype(jnp.float32),
        lax.psum_scatter(
            dense_grads[6].astype(jnp.bfloat16), "ctx", scatter_dimension=0, tiled=True
        ).astype(jnp.float32),
        lax.psum_scatter(
            dense_grads[7].astype(jnp.bfloat16), "ctx", scatter_dimension=0, tiled=True
        ).astype(jnp.float32),
    )
    expert_owned = (
        lax.psum_scatter(
            expert_grads[0].astype(jnp.bfloat16), "ctx", scatter_dimension=1, tiled=True
        ).astype(jnp.float32),
        lax.psum_scatter(
            expert_grads[1].astype(jnp.bfloat16), "ctx", scatter_dimension=1, tiled=True
        ).astype(jnp.float32),
        lax.psum_scatter(
            expert_grads[2].astype(jnp.bfloat16), "ctx", scatter_dimension=1, tiled=True
        ).astype(jnp.float32),
    )
    return (tuple(dense_owned), tuple(expert_owned))


def add_all(earlier, latest):
    if earlier is None:
        return latest
    return tuple((first_one + second_one for first_one, second_one in zip(earlier, latest)))


def attend_forward(query, key_rows, value_rows):
    batch_count, query_count, head_count, head_size = query.shape

    def add_piece(state_pair, pieces, offset):
        key_piece = pieces[0].reshape(batch_count, -1, head_count, head_size)
        value_piece = pieces[1].reshape(batch_count, -1, head_count, head_size)
        scores = jnp.einsum("bqhd,bkhd->bhqk", query, key_piece, preferred_element_type=jnp.float32)
        exponent = jnp.exp(scores)
        denominator = jnp.sum(exponent, axis=-1)
        accum_sum = jnp.einsum(
            "bhqk,bkhd->bqhd",
            exponent.astype(jnp.bfloat16),
            value_piece,
            preferred_element_type=jnp.float32,
        )
        return (accum_sum, denominator)

    initial = (
        jnp.zeros(query.shape, jnp.float32),
        jnp.zeros((batch_count, head_count, query_count), jnp.float32),
    )
    return add_piece(
        initial,
        (
            lax.all_gather(key_rows, "ctx", axis=1, tiled=True),
            lax.all_gather(value_rows, "ctx", axis=1, tiled=True),
        ),
        jnp.int32(0),
    )


def attend_backward(query, key_rows, value_rows, grad_acc, grad_total):
    batch_count, query_count, head_count, head_size = query.shape
    full_len = key_rows.shape[1] * lax.axis_size("ctx")

    def add_piece(state_three, pieces, offset):
        key_piece = pieces[0].reshape(batch_count, -1, head_count, head_size)
        value_piece = pieces[1].reshape(batch_count, -1, head_count, head_size)
        piece_len = key_piece.shape[1]
        scores = jnp.einsum("bqhd,bkhd->bhqk", query, key_piece, preferred_element_type=jnp.float32)
        exponent = jnp.exp(scores)
        grad_prob = jnp.einsum(
            "bqhd,bkhd->bhqk", grad_acc, value_piece, preferred_element_type=jnp.float32
        )
        grad_score = (exponent * (grad_prob + grad_total[..., None])).astype(jnp.bfloat16)
        grad_query = jnp.einsum(
            "bhqk,bkhd->bqhd", grad_score, key_piece, preferred_element_type=jnp.float32
        )
        key_term = jnp.einsum(
            "bhqk,bqhd->bkhd", grad_score, query, preferred_element_type=jnp.float32
        ).reshape(batch_count, piece_len, -1)
        value_term = jnp.einsum(
            "bhqk,bqhd->bkhd",
            exponent.astype(jnp.bfloat16),
            grad_acc,
            preferred_element_type=jnp.float32,
        ).reshape(batch_count, piece_len, -1)
        return (grad_query, key_term, value_term)

    initial = (jnp.zeros(query.shape, jnp.float32),)
    initial = initial + (
        jnp.zeros((batch_count, full_len, head_count * head_size), jnp.float32),
        jnp.zeros((batch_count, full_len, head_count * head_size), jnp.float32),
    )
    return add_piece(
        initial,
        (
            lax.all_gather(key_rows, "ctx", axis=1, tiled=True),
            lax.all_gather(value_rows, "ctx", axis=1, tiled=True),
        ),
        jnp.int32(0),
    )


def dispatch(route_block, gate_item, expert_count):
    group_count, local_len, chosen_count = route_block.shape
    expert_ids = route_block.reshape(group_count, local_len * chosen_count)
    onehot = (expert_ids[..., None] == jnp.arange(expert_count)[None, None, :]).astype(jnp.int32)
    before = jnp.cumsum(onehot, axis=1) - onehot
    position = jnp.sum(before * onehot, axis=2)
    slot_index = (
        expert_ids * (group_count * MOST) + jnp.arange(group_count)[:, None] * MOST + position
    )
    owner_row = (
        jnp.arange(group_count)[:, None] * local_len
        + jnp.arange(local_len * chosen_count)[None, :] // chosen_count
    )
    slot_index = slot_index.reshape(-1)
    source_rows = (
        jnp.zeros(expert_count * group_count * MOST, jnp.int32)
        .at[slot_index]
        .set(owner_row.reshape(-1))
    )
    gate_slot = (
        jnp.zeros(expert_count * group_count * MOST, jnp.float32)
        .at[slot_index]
        .set(gate_item.reshape(-1))
    )
    return (slot_index, source_rows, gate_slot)


def per_device(
    tokens,
    cotangent,
    routes,
    attn_gain,
    ffn_gain,
    qk_gain,
    w_query,
    w_key,
    w_value,
    w_out,
    router,
    w_gate,
    w_up,
    w_down,
):
    sequences, local_len, model_width = tokens.shape
    head_size = qk_gain.shape[0] * lax.axis_size("ctx")
    head_count = w_query.shape[1] // head_size
    expert_count = w_gate.shape[0]
    chosen_count = routes.shape[2]
    group_count = sequences // MICRO
    row_count = group_count * local_len
    half_size = head_size // 2
    positions = (lax.axis_index("ctx") * local_len + jnp.arange(local_len)).astype(jnp.float32)
    frequencies = ROPE_BASE ** (-2.0 * jnp.arange(half_size).astype(jnp.float32) / head_size)
    angles = positions[:, None] * frequencies[None, :]
    cosines = jnp.cos(angles)[None, :, None, :]
    sines = jnp.sin(angles)[None, :, None, :]
    score_scale = head_size ** (-0.5)
    shape_heads = (group_count, local_len, head_count, head_size)
    dense_total = None
    expert_total = None
    out_parts = []
    grad_parts = []
    for micro_step in range(MICRO):
        first_seq = micro_step * group_count
        inputs = (
            tokens[first_seq : first_seq + group_count]
            .astype(jnp.float32)
            .reshape(row_count, model_width)
        )
        route_block = routes[first_seq : first_seq + group_count]
        upstream = (
            cotangent[first_seq : first_seq + group_count]
            .astype(jnp.float32)
            .reshape(row_count, model_width)
        )
        gain_attn, gain_ffn, gain_qk, full_query, full_key, full_value, full_out, full_router = (
            fetch_dense(attn_gain, ffn_gain, qk_gain, w_query, w_key, w_value, w_out, router)
        )
        full_gate, full_up, full_down = fetch_experts(w_gate, w_up, w_down)
        attn_vec = gain_attn.astype(jnp.float32)
        ffn_vec = gain_ffn.astype(jnp.float32)
        query_gain = gain_qk[:, 0].astype(jnp.float32)
        key_gain = gain_qk[:, 1].astype(jnp.float32)
        scale_one = inverse_rms(inputs)
        normed = (inputs * scale_one * attn_vec).astype(jnp.bfloat16)
        query_lin = product(normed, full_query).reshape(shape_heads)
        key_lin = product(normed, full_key).reshape(shape_heads)
        value_send = (
            product(normed, full_value).astype(jnp.bfloat16).reshape(group_count, local_len, -1)
        )
        query_scale = inverse_rms(query_lin)
        key_scale = inverse_rms(key_lin)
        query_hat = query_lin * query_scale
        key_hat = key_lin * key_scale
        query = (rotate(query_hat * query_gain, cosines, sines) * score_scale).astype(jnp.bfloat16)
        key_rows = (
            rotate(key_hat * key_gain, cosines, sines)
            .astype(jnp.bfloat16)
            .reshape(group_count, local_len, -1)
        )
        accum_sum, denominator = attend_forward(query, key_rows, value_send)
        per_row_total = jnp.transpose(denominator, (0, 2, 1))[..., None]
        attended = accum_sum / per_row_total
        attended_low = attended.astype(jnp.bfloat16).reshape(row_count, -1)
        branch = lax.psum(
            jnp.einsum("nc,dc->nd", attended_low, full_out, preferred_element_type=jnp.float32),
            "tp",
        )
        middle = inputs + branch
        scale_two = inverse_rms(middle)
        normed_ffn = (middle * scale_two * ffn_vec).astype(jnp.bfloat16)
        logits = product(normed_ffn, full_router)
        probs = jax.nn.softmax(logits, axis=-1)
        route_flat = route_block.reshape(row_count, chosen_count)
        picked = (route_flat[:, :, None] == jnp.arange(expert_count)[None, None, :]).astype(
            jnp.float32
        )
        gate_item = jnp.sum(picked * probs[:, None, :], axis=-1)
        slot_index, source_rows, gate_slot = dispatch(route_block, gate_item, expert_count)
        expert_in = normed_ffn[source_rows].reshape(expert_count, -1, model_width)
        gate_pre = jnp.einsum(
            "erd,edf->erf", expert_in, full_gate, preferred_element_type=jnp.float32
        )
        up_pre = jnp.einsum("erd,edf->erf", expert_in, full_up, preferred_element_type=jnp.float32)
        activated = jax.nn.silu(gate_pre) * up_pre
        gate_col = gate_slot.reshape(expert_count, -1)[:, :, None]
        hidden = (gate_col * activated).astype(jnp.bfloat16)
        expert_out = jnp.einsum(
            "erf,edf->erd", hidden, full_down, preferred_element_type=jnp.float32
        )
        mixed_part = (
            jnp.zeros((row_count, model_width), jnp.float32)
            .at[source_rows]
            .add(expert_out.reshape(-1, model_width))
        )
        mixed = lax.psum(mixed_part.astype(jnp.bfloat16), "tp").astype(jnp.float32)
        out_parts.append(
            (middle + mixed).astype(jnp.bfloat16).reshape(group_count, local_len, model_width)
        )
        gain_attn, gain_ffn, gain_qk, full_query, full_key, full_value, full_out, full_router = (
            fetch_dense(attn_gain, ffn_gain, qk_gain, w_query, w_key, w_value, w_out, router)
        )
        full_gate, full_up, full_down = fetch_experts(w_gate, w_up, w_down)
        grad_mixed = upstream.astype(jnp.bfloat16)
        grad_rows = grad_mixed[source_rows].reshape(expert_count, -1, model_width)
        grad_down_w = jnp.einsum(
            "erd,erf->edf", grad_rows, hidden, preferred_element_type=jnp.float32
        )
        grad_hidden = jnp.einsum(
            "erd,edf->erf", grad_rows, full_down, preferred_element_type=jnp.float32
        )
        gate_slot_grad = jnp.sum(grad_hidden * activated, axis=-1)
        grad_act = gate_col * grad_hidden
        sigmoid_gate = jax.nn.sigmoid(gate_pre)
        grad_up_pre = (grad_act * jax.nn.silu(gate_pre)).astype(jnp.bfloat16)
        grad_gate_pre = (
            grad_act * up_pre * sigmoid_gate * (1.0 + gate_pre * (1.0 - sigmoid_gate))
        ).astype(jnp.bfloat16)
        grad_gate_w = jnp.einsum(
            "erd,erf->edf", expert_in, grad_gate_pre, preferred_element_type=jnp.float32
        )
        grad_up_w = jnp.einsum(
            "erd,erf->edf", expert_in, grad_up_pre, preferred_element_type=jnp.float32
        )
        grad_in = jnp.einsum(
            "erf,edf->erd", grad_gate_pre, full_gate, preferred_element_type=jnp.float32
        ) + jnp.einsum("erf,edf->erd", grad_up_pre, full_up, preferred_element_type=jnp.float32)
        grad_normed_part = (
            jnp.zeros((row_count, model_width), jnp.float32)
            .at[source_rows]
            .add(grad_in.reshape(-1, model_width))
        )
        gate_grad_part = gate_slot_grad.reshape(-1)[slot_index].reshape(row_count, chosen_count)
        gate_grad = lax.psum(gate_grad_part, "tp")
        grad_probs = jnp.sum(picked * gate_grad[:, :, None], axis=1)
        grad_logits = (
            probs * (grad_probs - jnp.sum(probs * grad_probs, axis=-1, keepdims=True))
        ).astype(jnp.bfloat16)
        grad_router = jnp.einsum(
            "nd,ne->de", normed_ffn, grad_logits, preferred_element_type=jnp.float32
        )
        grad_normed = lax.psum(grad_normed_part, "tp") + jnp.einsum(
            "ne,de->nd", grad_logits, full_router, preferred_element_type=jnp.float32
        )
        grad_ffn_gain = jnp.sum(grad_normed * (middle * scale_two), axis=0)
        grad_middle = upstream + norm_back(grad_normed, middle, scale_two, ffn_vec)
        grad_branch = grad_middle.astype(jnp.bfloat16)
        grad_out_w = jnp.einsum(
            "nd,nc->dc", grad_branch, attended_low, preferred_element_type=jnp.float32
        )
        grad_att = jnp.einsum(
            "nd,dc->nc", grad_branch, full_out, preferred_element_type=jnp.float32
        ).reshape(shape_heads)
        grad_acc = (grad_att / per_row_total).astype(jnp.bfloat16)
        grad_total = jnp.transpose(-jnp.sum(grad_att * attended, axis=-1), (0, 2, 1)) / denominator
        grad_query, key_full, value_full = attend_backward(
            query, key_rows, value_send, grad_acc, grad_total
        )
        grad_keys, grad_values = (
            lax.psum_scatter(
                key_full.astype(jnp.bfloat16), "ctx", scatter_dimension=1, tiled=True
            ).astype(jnp.float32),
            lax.psum_scatter(
                value_full.astype(jnp.bfloat16), "ctx", scatter_dimension=1, tiled=True
            ).astype(jnp.float32),
        )
        grad_value_lin = grad_values.astype(jnp.bfloat16).reshape(row_count, -1)
        key_norm_grad = rotate(grad_keys.reshape(shape_heads), cosines, -sines)
        query_norm_grad = rotate(grad_query * score_scale, cosines, -sines)
        grad_qk_part = jnp.stack(
            [
                jnp.sum(query_norm_grad * query_hat, axis=(0, 1, 2)),
                jnp.sum(key_norm_grad * key_hat, axis=(0, 1, 2)),
            ],
            axis=1,
        )
        grad_query_lin = (
            norm_back(query_norm_grad, query_lin, query_scale, query_gain)
            .astype(jnp.bfloat16)
            .reshape(row_count, -1)
        )
        grad_key_lin = (
            norm_back(key_norm_grad, key_lin, key_scale, key_gain)
            .astype(jnp.bfloat16)
            .reshape(row_count, -1)
        )
        grad_query_w = jnp.einsum(
            "nd,nc->dc", normed, grad_query_lin, preferred_element_type=jnp.float32
        )
        grad_key_w = jnp.einsum(
            "nd,nc->dc", normed, grad_key_lin, preferred_element_type=jnp.float32
        )
        grad_value_w = jnp.einsum(
            "nd,nc->dc", normed, grad_value_lin, preferred_element_type=jnp.float32
        )
        grad_normed_attn = jnp.einsum(
            "nc,dc->nd", grad_query_lin, full_query, preferred_element_type=jnp.float32
        )
        grad_normed_attn = grad_normed_attn + jnp.einsum(
            "nc,dc->nd", grad_key_lin, full_key, preferred_element_type=jnp.float32
        )
        grad_normed_attn = grad_normed_attn + jnp.einsum(
            "nc,dc->nd", grad_value_lin, full_value, preferred_element_type=jnp.float32
        )
        grad_normed_one, grad_qk = (
            lax.psum(grad_normed_attn.astype(jnp.bfloat16), "tp").astype(jnp.float32),
            lax.psum(grad_qk_part.astype(jnp.bfloat16), "tp").astype(jnp.float32),
        )
        grad_attn_gain = jnp.sum(grad_normed_one * (inputs * scale_one), axis=0)
        grad_inputs = grad_middle + norm_back(grad_normed_one, inputs, scale_one, attn_vec)
        grad_parts.append(
            grad_inputs.astype(jnp.bfloat16).reshape(group_count, local_len, model_width)
        )
        dense_grads = (
            grad_attn_gain,
            grad_ffn_gain,
            grad_qk,
            grad_query_w,
            grad_key_w,
            grad_value_w,
            grad_out_w,
            grad_router,
        )
        expert_grads = (grad_gate_w, grad_up_w, grad_down_w)
        dense_total = add_all(dense_total, dense_grads)
        expert_total = add_all(expert_total, expert_grads)
    dense_owned, expert_owned = reduce_grads(dense_total, expert_total)
    layer_out = jnp.concatenate(out_parts, axis=0)
    input_grad = jnp.concatenate(grad_parts, axis=0)
    return (layer_out, input_grad) + tuple(dense_owned) + tuple(expert_owned)


def solution(mesh):
    return jax.shard_map(
        per_device,
        mesh=mesh,
        in_specs=(
            P(None, "ctx", None),
            P(None, "ctx", None),
            P(None, "ctx", None),
            P("ctx"),
            P("ctx"),
            P("ctx", None),
            P("ctx", "tp"),
            P("ctx", "tp"),
            P("ctx", "tp"),
            P("ctx", "tp"),
            P("ctx", None),
            P(None, "ctx", "tp"),
            P(None, "ctx", "tp"),
            P(None, "ctx", "tp"),
        ),
        out_specs=(
            P(None, "ctx", None),
            P(None, "ctx", None),
            P("ctx"),
            P("ctx"),
            P("ctx", None),
            P("ctx", "tp"),
            P("ctx", "tp"),
            P("ctx", "tp"),
            P("ctx", "tp"),
            P("ctx", None),
            P(None, "ctx", "tp"),
            P(None, "ctx", "tp"),
            P(None, "ctx", "tp"),
        ),
        check_vma=False,
    )
```

profile of v0, /device:TPU:29, one launch (start us, length us, event | category | flops | bytes accessed | tf_op | source)
XLA Modules:
  0.0 2948.7 jit_solution(5728005083713232444)
XLA Ops:
  63.0 46.0 %all-gather.19.cloned.1.call-done = bf16[2048,512]{1,0:T(8,128)(2,1)} async-done(((bf16[256,512]{1,0:T(8,128)(2,1)}), bf16[2048,512]{1,0:T(8,128)(2,1)}) %all-gather.19.cloned.1.call-update) | async-done | bytes 2097168 | tf_op jit(solution)/shard_map/all_gather | solution.py:44
  127.0 32.1 %all-gather.15.cloned.1.call-done = bf16[2048,512]{1,0:T(8,128)(2,1)} async-done(((bf16[256,512]{1,0:T(8,128)(2,1)}), bf16[2048,512]{1,0:T(8,128)(2,1)}) %all-gather.15.cloned.1.call-update) | async-done | bytes 2097168 | tf_op jit(solution)/shard_map/all_gather | solution.py:46
  167.8 31.1 %all-gather.35.cloned.1.call-done = bf16[2,512,512]{2,1,0:T(8,128)(2,1)} async-done(((bf16[2,64,512]{2,1,0:T(8,128)(2,1)}), bf16[2,512,512]{2,1,0:T(8,128)(2,1)}) %all-gather.35.cloned.1.call-update) | async-done | bytes 1048592 | tf_op jit(solution)/shard_map/all_gather | solution.py:131
  200.4 40.0 %all-gather.33.cloned.1.call-done = bf16[2,512,512]{2,0,1:T(2,128)(2,1)} async-done(((bf16[2,64,512]{2,0,1:T(2,128)(2,1)}), bf16[2,512,512]{2,0,1:T(2,128)(2,1)}) %all-gather.33.cloned.1.call-update) | async-done | bytes 1048592 | tf_op jit(solution)/shard_map/all_gather | solution.py:132
  245.5 36.4 %all-gather.23.cloned.1.call-done = bf16[2,512,512]{2,1,0:T(8,128)(2,1)} async-done(((bf16[2,64,512]{2,1,0:T(8,128)(2,1)}), bf16[2,512,512]{2,1,0:T(8,128)(2,1)}) %all-gather.23.cloned.1.call-update) | async-done | bytes 1048592 | tf_op jit(solution)/shard_map/all_gather | solution.py:131
  283.5 40.1 %all-gather.17.cloned.1.call-done = bf16[2,512,512]{2,0,1:T(2,128)(2,1)} async-done(((bf16[2,64,512]{2,0,1:T(2,128)(2,1)}), bf16[2,512,512]{2,0,1:T(2,128)(2,1)}) %all-gather.17.cloned.1.call-update) | async-done | bytes 1048592 | tf_op jit(solution)/shard_map/all_gather | solution.py:132
  328.7 46.6 %all-gather.25.cloned.1.call-done = bf16[2048,512]{1,0:T(8,128)(2,1)} async-done(((bf16[256,512]{1,0:T(8,128)(2,1)}), bf16[2048,512]{1,0:T(8,128)(2,1)}) %all-gather.25.cloned.1.call-update) | async-done | bytes 2097168 | tf_op jit(solution)/shard_map/all_gather | solution.py:47
  434.4 26.9 all_gather.39
  479.7 181.5 %all-gather.29.cloned.1.call-done = bf16[16,2048,256]{2,1,0:T(8,128)(2,1)} async-done(((bf16[16,256,256]{2,1,0:T(8,128)(2,1)}), bf16[16,2048,256]{2,1,0:T(8,128)(2,1)}) %all-gather.29.cloned.1.call-update) | async-done | bytes 16777232 | tf_op jit(solution)/shard_map/all_gather | solution.py:55
  671.5 217.9 %all-gather.27.cloned.1.call-done = bf16[16,2048,256]{2,1,0:T(8,128)(2,1)} async-done(((bf16[16,256,256]{2,1,0:T(8,128)(2,1)}), bf16[16,2048,256]{2,1,0:T(8,128)(2,1)}) %all-gather.27.cloned.1.call-update) | async-done | bytes 16777232 | tf_op jit(solution)/shard_map/all_gather | solution.py:54
  899.8 217.7 %all-gather.31.cloned.1.call-done = bf16[16,2048,256]{2,1,0:T(8,128)(2,1)} async-done(((bf16[16,256,256]{2,1,0:T(8,128)(2,1)}), bf16[16,2048,256]{2,1,0:T(8,128)(2,1)}) %all-gather.31.cloned.1.call-update) | async-done | bytes 16777232 | tf_op jit(solution)/shard_map/all_gather | solution.py:56
  1302.5 50.4 %all-reduce.12.cloned.1.call-done = (f32[128,2048]{1,0:T(8,128)}, f32[128,2048]{1,0:T(8,128)}) async-done(((f32[128,2048]{1,0:T(8,128)}, f32[128,2048]{1,0:T(8,128)}), (f32[128,2048]{1,0:T(8,128)}, f32[128,2048]{1,0:T(8,128)})) %all-reduce.12.cloned.1.call-update) | async-done | bytes 2097168 | tf_op jit(solution)/shard_map/psum | solution.py:362
  1427.1 22.0 scatter_custom_fusion.2
  1457.0 41.0 %reduce-scatter.20.cloned.1.call-done = bf16[2,64,512]{2,1,0:T(8,128)(2,1)} async-done(((bf16[2,512,512]{2,1,0:T(8,128)(2,1)}), bf16[2,64,512]{2,1,0:T(8,128)(2,1)}) %reduce-scatter.20.cloned.1.call-update) | async-done | bytes 131088 | tf_op jit(solution)/shard_map/reduce_scatter | solution.py:380
  1516.6 47.8 %reduce-scatter.22.cloned.1.call-done = bf16[2,64,512]{2,1,0:T(8,128)(2,1)} async-done(((bf16[2,512,512]{2,1,0:T(8,128)(2,1)}), bf16[2,64,512]{2,1,0:T(8,128)(2,1)}) %reduce-scatter.22.cloned.1.call-update) | async-done | bytes 131088 | tf_op jit(solution)/shard_map/reduce_scatter | solution.py:383
  1568.9 61.7 %reduce-scatter.18.cloned.1.call-done = bf16[2,64,512]{2,1,0:T(8,128)(2,1)} async-done(((bf16[2,512,512]{2,1,0:T(8,128)(2,1)}), bf16[2,64,512]{2,1,0:T(8,128)(2,1)}) %reduce-scatter.18.cloned.1.call-update) | async-done | bytes 131088 | tf_op jit(solution)/shard_map/reduce_scatter | solution.py:383
  1767.7 30.8 %all-reduce.16.cloned.1.call-done = (bf16[128,2048]{1,0:T(8,128)(2,1)}, bf16[128,2048]{1,0:T(8,128)(2,1)}, bf16[128,2048]{1,0:T(8,128)(2,1)}, bf16[128,2048]{1,0:T(8,128)(2,1)}) async-done(((bf16[128,2048]{1,0:T(8,128)(2,1)}, bf16[128,2048]{1,0:T(8,128)(2,1)}, bf16[128,2048]{1,0:T(8,128)(2,1)}, bf16[128,2048]{1,0:T(8,128)(2,1)}), (bf16[128,2048]{1,0:T(8,128)(2,1)}, bf16[128,2048]{1,0:T(8,128)(2,1)}, ...) | async-done | bytes 2097168 | tf_op jit(solution)/shard_map/psum | solution.py:316
  1821.8 46.2 %reduce-scatter.30.cloned.1.call-done = bf16[256,512]{1,0:T(8,128)(2,1)} async-done(((bf16[2048,512]{1,0:T(8,128)(2,1)}), bf16[256,512]{1,0:T(8,128)(2,1)}) %reduce-scatter.30.cloned.1.call-update) | async-done | bytes 262160 | tf_op jit(solution)/shard_map/reduce_scatter | solution.py:80
  1869.8 69.4 %reduce-scatter.24.cloned.1.call-done = bf16[256,512]{1,0:T(8,128)(2,1)} async-done(((bf16[2048,512]{1,0:T(8,128)(2,1)}), bf16[256,512]{1,0:T(8,128)(2,1)}) %reduce-scatter.24.cloned.1.call-update) | async-done | bytes 262160 | tf_op jit(solution)/shard_map/reduce_scatter | solution.py:71
  1940.9 69.4 %reduce-scatter.26.cloned.1.call-done = bf16[256,512]{1,0:T(8,128)(2,1)} async-done(((bf16[2048,512]{1,0:T(8,128)(2,1)}), bf16[256,512]{1,0:T(8,128)(2,1)}) %reduce-scatter.26.cloned.1.call-update) | async-done | bytes 262160 | tf_op jit(solution)/shard_map/reduce_scatter | solution.py:74
  2012.1 69.3 %reduce-scatter.28.cloned.1.call-done = bf16[256,512]{1,0:T(8,128)(2,1)} async-done(((bf16[2048,512]{1,0:T(8,128)(2,1)}), bf16[256,512]{1,0:T(8,128)(2,1)}) %reduce-scatter.28.cloned.1.call-update) | async-done | bytes 262160 | tf_op jit(solution)/shard_map/reduce_scatter | solution.py:77
  2083.2 284.7 %reduce-scatter.34.cloned.1.call-done = bf16[16,256,256]{2,1,0:T(8,128)(2,1)} async-done(((bf16[16,2048,256]{2,1,0:T(8,128)(2,1)}), bf16[16,256,256]{2,1,0:T(8,128)(2,1)}) %reduce-scatter.34.cloned.1.call-update) | async-done | bytes 2097168 | tf_op jit(solution)/shard_map/reduce_scatter | solution.py:88
  2371.9 280.6 %reduce-scatter.36.cloned.1.call-done = bf16[16,256,256]{2,1,0:T(8,128)(2,1)} async-done(((bf16[16,2048,256]{2,1,0:T(8,128)(2,1)}), bf16[16,256,256]{2,1,0:T(8,128)(2,1)}) %reduce-scatter.36.cloned.1.call-update) | async-done | bytes 2097168 | tf_op jit(solution)/shard_map/reduce_scatter | solution.py:91
  2656.6 281.0 %reduce-scatter.38.cloned.1.call-done = bf16[16,256,256]{2,1,0:T(8,128)(2,1)} async-done(((bf16[16,2048,256]{2,1,0:T(8,128)(2,1)}), bf16[16,256,256]{2,1,0:T(8,128)(2,1)}) %reduce-scatter.38.cloned.1.call-update) | async-done | bytes 2097168 | tf_op jit(solution)/shard_map/reduce_scatter | solution.py:94
  (586 shorter events, 660.6 us)
Async XLA Ops:
  8.7 150.4 %all-gather.15.cloned.1.call-start = ((), (), s32[]{:S(2)}) async-start(), calls=%async_computation.13 | async-start | bytes 2359296 | tf_op jit(solution)/shard_map/all_gather | solution.py:46
  9.4 189.5 %all-gather.35.cloned.1.call-start = ((), (), s32[]{:S(2)}) async-start(), calls=%async_computation.23 | async-start | bytes 1179648 | tf_op jit(solution)/shard_map/all_gather | solution.py:131
  162.0 120.0 %all-gather.23.cloned.1.call-start = ((), (), s32[]{:S(2)}) async-start(), calls=%async_computation.17 | async-start | bytes 1179648 | tf_op jit(solution)/shard_map/all_gather | solution.py:131
  163.7 159.9 %all-gather.17.cloned.1.call-start = ((), (), s32[]{:S(2)}) async-start(), calls=%async_computation.14 | async-start | bytes 1179648 | tf_op jit(solution)/shard_map/all_gather | solution.py:132
  166.6 208.7 %all-gather.25.cloned.1.call-start = ((), (), s32[]{:S(2)}) async-start(), calls=%async_computation.18 | async-start | bytes 2359296 | tf_op jit(solution)/shard_map/all_gather | solution.py:47
  167.4 294.0 %all-reduce.14.cloned.1.call-start = ((), (), s32[]{:S(2)}) async-start(), calls=%async_computation.38 | async-start | bytes 4194304 | tf_op jit(solution)/shard_map/psum | solution.py:285
  380.7 280.5 %all-gather.29.cloned.1.call-start = ((), (), s32[]{:S(2)}) async-start(), calls=%async_computation.20 | async-start | bytes 18874368 | tf_op jit(solution)/shard_map/all_gather | solution.py:55
  381.3 508.1 %all-gather.27.cloned.1.call-start = ((), (), s32[]{:S(2)}) async-start(), calls=%async_computation.19 | async-start | bytes 18874368 | tf_op jit(solution)/shard_map/all_gather | solution.py:54
  382.0 735.5 %all-gather.31.cloned.1.call-start = ((), (), s32[]{:S(2)}) async-start(), calls=%async_computation.21 | async-start | bytes 18874368 | tf_op jit(solution)/shard_map/all_gather | solution.py:56
  382.6 970.3 %all-reduce.12.cloned.1.call-start = ((), (), s32[]{:S(2)}) async-start(), calls=%async_computation.37 | async-start | bytes 4194304 | tf_op jit(solution)/shard_map/psum | solution.py:362
  1302.1 153.6 %reduce-scatter.16.cloned.1.call-start = ((), (), s32[]{:S(2)}) async-start(), calls=%async_computation.24 | async-start | bytes 1179648 | tf_op jit(solution)/shard_map/reduce_scatter | solution.py:380
  1369.5 128.6 %reduce-scatter.20.cloned.1.call-start = ((), (), s32[]{:S(2)}) async-start(), calls=%async_computation.26 | async-start | bytes 1179648 | tf_op jit(solution)/shard_map/reduce_scatter | solution.py:380
  1377.0 187.4 %reduce-scatter.22.cloned.1.call-start = ((), (), s32[]{:S(2)}) async-start(), calls=%async_computation.27 | async-start | bytes 1179648 | tf_op jit(solution)/shard_map/reduce_scatter | solution.py:383
  1379.2 251.4 %reduce-scatter.18.cloned.1.call-start = ((), (), s32[]{:S(2)}) async-start(), calls=%async_computation.25 | async-start | bytes 1179648 | tf_op jit(solution)/shard_map/reduce_scatter | solution.py:383
  1415.4 349.6 %reduce-scatter.32.cloned.1.call-start = ((), (), s32[]{:S(2)}) async-start(), calls=%async_computation.32 | async-start | bytes 73728 | tf_op jit(solution)/shard_map/reduce_scatter | solution.py:83
  1452.3 314.1 %reduce-scatter.40.cloned.1.call-start = ((), (), s32[]{:S(2)}) async-start(), calls=%async_computation.36 | async-start | bytes 36864
  1510.7 287.8 %all-reduce.16.cloned.1.call-start = ((), (), s32[]{:S(2)}) async-start(), calls=%async_computation.39 | async-start | bytes 4194304 | tf_op jit(solution)/shard_map/psum | solution.py:316
  1633.6 234.4 %reduce-scatter.30.cloned.1.call-start = ((), (), s32[]{:S(2)}) async-start(), calls=%async_computation.31 | async-start | bytes 2359296 | tf_op jit(solution)/shard_map/reduce_scatter | solution.py:80
  1637.5 301.7 %reduce-scatter.24.cloned.1.call-start = ((), (), s32[]{:S(2)}) async-start(), calls=%async_computation.28 | async-start | bytes 2359296 | tf_op jit(solution)/shard_map/reduce_scatter | solution.py:71
  1640.6 369.7 %reduce-scatter.26.cloned.1.call-start = ((), (), s32[]{:S(2)}) async-start(), calls=%async_computation.29 | async-start | bytes 2359296 | tf_op jit(solution)/shard_map/reduce_scatter | solution.py:74
  1643.4 438.0 %reduce-scatter.28.cloned.1.call-start = ((), (), s32[]{:S(2)}) async-start(), calls=%async_computation.30 | async-start | bytes 2359296 | tf_op jit(solution)/shard_map/reduce_scatter | solution.py:77
  1646.4 721.5 %reduce-scatter.34.cloned.1.call-start = ((), (), s32[]{:S(2)}) async-start(), calls=%async_computation.33 | async-start | bytes 18874368 | tf_op jit(solution)/shard_map/reduce_scatter | solution.py:88
  1684.9 967.7 %reduce-scatter.36.cloned.1.call-start = ((), (), s32[]{:S(2)}) async-start(), calls=%async_computation.34 | async-start | bytes 18874368 | tf_op jit(solution)/shard_map/reduce_scatter | solution.py:91
  1723.9 1213.7 %reduce-scatter.38.cloned.1.call-start = ((), (), s32[]{:S(2)}) async-start(), calls=%async_computation.35 | async-start | bytes 18874368 | tf_op jit(solution)/shard_map/reduce_scatter | solution.py:94
  (141 other events, 4315.7 us)
Sparse Core Ops, SparseCore 0:
  10.1 48.9 all-gather.20
  61.3 47.7 all-gather.18
  111.2 47.8 all-gather.14
  243.0 38.9 all-gather.22
  325.7 49.5 all-gather.24
  380.8 50.9 all-reduce.13
  434.0 227.1 all-gather.28
  663.6 225.7 all-gather.26
  891.7 225.7 all-gather.30
  1302.2 50.6 all-reduce.11
  1369.6 61.6 reduce-scatter.15
  1435.5 62.5 reduce-scatter.19
  1501.9 62.5 reduce-scatter.21
  1568.1 62.4 reduce-scatter.17
  1633.6 52.2 reduce-scatter.31
  1689.0 52.5 reduce-scatter.39
  1745.1 53.3 all-reduce.15
  1802.5 65.4 reduce-scatter.29
  1872.5 66.5 reduce-scatter.23
  1943.7 66.6 reduce-scatter.25
  2014.7 66.6 reduce-scatter.27
  2085.7 282.1 reduce-scatter.33
  2371.5 281.0 reduce-scatter.35
  2656.7 280.9 reduce-scatter.37
  (3 shorter events, 114.7 us)
where the time goes:
time: 2960 us; the launch traced here: 2950 us
  waiting for transfers between devices  2250 us (76%)
  matrix products  320 us (11%)
  other arithmetic  155 us (5%)
  blocking collectives  109 us (4%)
  local copies, waits for them, and re-layouts  99.1 us (3%)
    reduce_scatter x1, waiting for transfers between devices, reduce_grads(): lax.psum_scatter(expert_grads[0].astype(jnp.bfloat16), 'ctx', scatter_dim...  285 us
    reduce_scatter x1, waiting for transfers between devices, reduce_grads(): lax.psum_scatter(expert_grads[2].astype(jnp.bfloat16), 'ctx', scatter_dim...  281 us
    reduce_scatter x1, waiting for transfers between devices, reduce_grads(): lax.psum_scatter(expert_grads[1].astype(jnp.bfloat16), 'ctx', scatter_dim...  281 us
    all_gather x1, waiting for transfers between devices, fetch_experts(): lax.all_gather(w_gate, 'ctx', axis=1, tiled=True)  218 us
    all_gather x1, waiting for transfers between devices, fetch_experts(): lax.all_gather(w_down, 'ctx', axis=1, tiled=True)  218 us
    all_gather x1, waiting for transfers between devices, fetch_experts(): lax.all_gather(w_up, 'ctx', axis=1, tiled=True)  182 us
    reduce_scatter x2, waiting for transfers between devices, per_device(): lax.psum_scatter(value_full.astype(jnp.bfloat16), 'ctx', scatter_dimensio...  110 us
    all_gather x2, waiting for transfers between devices, attend_forward(): lax.all_gather(value_rows, 'ctx', axis=1, tiled=True)  80.1 us
  transfers between devices with their start and end apart: 27, of which 23 were waited for; matrix products, arithmetic and copies ran while one was open for 13% of the time, Pallas kernels for 0%

commit v1 on v0

--- a/solution.py
+++ b/solution.py
@@ -450,9 +450,279 @@
     return (layer_out, input_grad) + tuple(dense_owned) + tuple(expert_owned)
 
 
+def xor_permute(array, mask):
+    return lax.ppermute(array, ("ctx", "tp"), [(i, i ^ mask) for i in range(32)])
+
+
+BIT_K, BIT_Y, BIT_X, BIT_Z1, BIT_Z2 = 1, 2, 4, 8, 16
+
+
+def with_partner(array, mask, axis):
+    return jnp.concatenate([array, xor_permute(array, mask)], axis=axis)
+
+
+def along_z(array, axis):
+    return jnp.concatenate(
+        [array] + [xor_permute(array, mask) for mask in (BIT_Z1, BIT_Z2, BIT_Z1 | BIT_Z2)], axis=axis
+    )
+
+
+def halve(array, mask, axis):
+    half = array.shape[axis] // 2
+    kept = lax.slice_in_dim(array, 0, half, axis=axis)
+    sent = lax.slice_in_dim(array, half, 2 * half, axis=axis)
+    return (kept.astype(jnp.float32) + xor_permute(sent, mask).astype(jnp.float32)).astype(jnp.bfloat16)
+
+
+def sum_z(array, axis):
+    size = array.shape[axis] // 4
+    parts = [lax.slice_in_dim(array, i * size, (i + 1) * size, axis=axis) for i in range(4)]
+    total = parts[0].astype(jnp.float32)
+    for i, mask in ((1, BIT_Z1), (2, BIT_Z2), (3, BIT_Z1 | BIT_Z2)):
+        total = total + xor_permute(parts[i], mask).astype(jnp.float32)
+    return total
+
+
+def gather_heads(owned):
+    return with_partner(with_partner(along_z(owned, 1), BIT_Y, 1), BIT_K, 1)
+
+
+def scatter_heads(partial):
+    return sum_z(halve(halve(partial, BIT_K, 1), BIT_Y, 1), 1)
+
+
+def gather_all(owned):
+    first = along_z(owned[0], 0)
+    second = along_z(owned[1], 0)
+    first = with_partner(with_partner(first, BIT_X, 0), BIT_Y, 0)
+    second = with_partner(with_partner(second, BIT_Y, 0), BIT_X, 0)
+    return with_partner(first, BIT_K, 0), with_partner(second, BIT_K, 0)
+
+
+def scatter_all(first, second):
+    first = halve(first, BIT_K, 0)
+    second = halve(second, BIT_K, 0)
+    first = halve(halve(first, BIT_Y, 0), BIT_X, 0)
+    second = halve(halve(second, BIT_X, 0), BIT_Y, 0)
+    return jnp.stack([sum_z(first, 0), sum_z(second, 0)], 0)
+
+
+def exchange(array):
+    return lax.all_to_all(array, "ctx", 0, 0, tiled=True)
+
+
+def per_device_fast(
+    tokens, cotangent, routes, attn_gain, ffn_gain, qk_gain, w_query, w_key, w_value, w_out, router, w_gate, w_up, w_down
+):
+    width = tokens.shape[2]
+    head_size = qk_gain.shape[0] * 8
+    half_size = head_size // 2
+    experts = w_gate.shape[0]
+    mine = experts // 8
+    hidden_units = w_gate.shape[2]
+    ctx, tp = lax.axis_index("ctx"), lax.axis_index("tp")
+    z, x, y, k = ctx // 2, ctx % 2, tp // 2, tp % 2
+    f32, bf16 = jnp.float32, jnp.bfloat16
+
+    pack = jnp.zeros((256, 20), bf16)
+    pack = pack.at[:, :experts].set(router).at[:, 16].set(attn_gain).at[:, 17].set(ffn_gain)
+    pack = pack.at[:16, 18:20].set(qk_gain)
+    pack = lax.all_gather(pack, "ctx", axis=0, tiled=True)
+    full_router = pack[:, :16]
+    attn_vec, ffn_vec = pack[:, 16].astype(f32), pack[:, 17].astype(f32)
+    qk_full = pack.reshape(8, 256, 20)[:, :16, 18:20].reshape(head_size, 2).astype(f32)
+    query_gain, key_gain = qk_full[:, 0], qk_full[:, 1]
+    all_routes = lax.all_gather(routes, "ctx", axis=1, tiled=True)
+
+    def own_rows(array):
+        rows = lax.dynamic_slice_in_dim(array, tp * 16, 16, 1)
+        kept = lax.dynamic_slice_in_dim(rows, 2 * x, 2, 0)
+        sent = lax.dynamic_slice_in_dim(rows, 2 - 2 * x, 2, 0)
+        return jnp.concatenate([kept, xor_permute(sent, BIT_X)], axis=1)
+
+    own_tokens = own_rows(tokens)
+    own_cot = own_rows(cotangent)
+    head_tokens = gather_heads(own_tokens)
+
+    dense = jnp.stack([w_query, w_key, w_value, w_out], 0).reshape(4, 256, 4, head_size)
+    dense = jnp.transpose(dense, (2, 1, 0, 3))
+    dense = jnp.repeat(dense, 2, axis=0)
+    dense = exchange(dense).reshape(width, 4, head_size)
+    w_qkv = dense[:, :3].reshape(width, 3 * head_size)
+    w_o = dense[:, 3]
+
+    def fetch(weight):
+        weight = exchange(weight.reshape(8, mine, 256, hidden_units))
+        return jnp.transpose(weight, (0, 2, 1, 3)).reshape(width, mine * hidden_units)
+
+    gate_w, up_w, down_w = fetch(w_gate), fetch(w_up), fetch(w_down)
+
+    cot_first, cot_second = gather_all(own_cot)
+    dm = jnp.concatenate([cot_first, cot_second], 0)
+
+    def bits(*shape):
+        return [lax.broadcasted_iota(jnp.int32, shape, i) for i in range(len(shape))]
+
+    dk, dy, dz, dx, i = bits(2, 2, 4, 2, 16)
+    positions = ((z ^ dz) * 2 + (x ^ dx)) * 64 + ((y ^ dy) * 2 + (k ^ dk)) * 16 + i
+    positions = positions.reshape(512).astype(f32)
+    frequencies = ROPE_BASE ** (-2.0 * jnp.arange(half_size).astype(f32) / head_size)
+    angles = positions[:, None] * frequencies[None, :]
+    cosines, sines = jnp.cos(angles)[None], jnp.sin(angles)[None]
+
+    def token_of(part, dx_dev, dy, dz, dk, dx_block, i):
+        return (2 * (x ^ dx_dev) + part) * 512 + ((z ^ dz) * 2 + (x ^ dx_dev ^ dx_block)) * 64 + ((y ^ dy) * 2 + (k ^ dk)) * 16 + i
+
+    dk, dy, dx, dz, db, i = bits(2, 2, 2, 4, 2, 16)
+    rows_first = token_of(0, dx, dy, dz, dk, db, i).reshape(-1)
+    dk, dx, dy, dz, db, i = bits(2, 2, 2, 4, 2, 16)
+    rows_second = token_of(1, dx, dy, dz, dk, db, i).reshape(-1)
+    row_tokens = jnp.concatenate([rows_first, rows_second], 0)
+    row_routes = jnp.take(all_routes.reshape(-1, routes.shape[2]), row_tokens, axis=0)
+    chosen = jnp.sum((row_routes[:, :, None] == jnp.arange(experts)[None, None, :]).astype(f32), axis=1)
+
+    inputs = head_tokens.astype(f32)
+    scale_one = inverse_rms(inputs)
+    unit = inputs * scale_one
+    normed = (unit * attn_vec).astype(bf16)
+    lin = product(normed, w_qkv)
+    query_lin, key_lin = lin[..., :head_size], lin[..., head_size : 2 * head_size]
+    value_rows = lin[..., 2 * head_size :].astype(bf16)
+    score_scale = head_size ** (-0.5)
+    query_scale, key_scale = inverse_rms(query_lin), inverse_rms(key_lin)
+    query_hat, key_hat = query_lin * query_scale, key_lin * key_scale
+    query = (rotate(query_hat * query_gain, cosines, sines) * score_scale).astype(bf16)
+    keys = rotate(key_hat * key_gain, cosines, sines).astype(bf16)
+    scores = jnp.einsum("sqd,skd->sqk", query, keys, preferred_element_type=f32)
+    exponent = jnp.exp(scores)
+    denominator = jnp.sum(exponent, axis=-1, keepdims=True)
+    expo_low = exponent.astype(bf16)
+    attended = jnp.einsum("sqk,skd->sqd", expo_low, value_rows, preferred_element_type=f32) / denominator
+    attended_low = attended.astype(bf16)
+    branch_part = jnp.einsum("snc,dc->snd", attended_low, w_o, preferred_element_type=f32).astype(bf16)
+    middle = own_tokens.astype(f32) + scatter_heads(branch_part)
+
+    scale_two = inverse_rms(middle)
+    unit_two = middle * scale_two
+    normed_ffn = (unit_two * ffn_vec).astype(bf16)
+    nf = jnp.concatenate(gather_all(normed_ffn), 0)
+    probs = jax.nn.softmax(product(nf, full_router), axis=-1)
+    own_probs = lax.dynamic_slice_in_dim(probs, mine * ctx, mine, 1)
+    own_chosen = lax.dynamic_slice_in_dim(chosen, mine * ctx, mine, 1)
+    gates = own_probs * own_chosen
+    rows = nf.shape[0]
+
+    def spread(columns):
+        return jnp.broadcast_to(columns[:, :, None], (rows, mine, hidden_units)).reshape(rows, mine * hidden_units)
+
+    gate_pre, up_pre = product(nf, gate_w), product(nf, up_w)
+    sigmoid_gate = jax.nn.sigmoid(gate_pre)
+    silu_gate = gate_pre * sigmoid_gate
+    activated = silu_gate * up_pre
+    gate_wide = spread(gates)
+    hidden = (gate_wide * activated).astype(bf16)
+    mixed_part = jnp.einsum("nf,df->nd", hidden, down_w, preferred_element_type=f32).astype(bf16)
+    half_rows = rows // 2
+    mixed = scatter_all(mixed_part[:half_rows], mixed_part[half_rows:])
+    layer_out = (middle + mixed).astype(bf16)
+
+    grad_hidden = product(dm, down_w)
+    gate_grad = jnp.sum((grad_hidden * activated).reshape(rows, mine, hidden_units), axis=-1) * own_chosen
+    grad_act = gate_wide * grad_hidden
+    grad_up_pre = (grad_act * silu_gate).astype(bf16)
+    grad_gate_pre = (grad_act * up_pre * sigmoid_gate * (1.0 + gate_pre * (1.0 - sigmoid_gate))).astype(bf16)
+    own_ids = mine * ctx + jnp.arange(mine)
+    placed = jnp.sum(gate_grad[:, :, None] * (own_ids[:, None] == jnp.arange(experts)[None, :]).astype(f32), axis=1)
+    grad_logits = (probs * (placed - jnp.sum(probs * placed, axis=-1, keepdims=True))).astype(bf16)
+    grad_normed_part = (
+        jnp.einsum("nf,df->nd", grad_gate_pre, gate_w, preferred_element_type=f32)
+        + jnp.einsum("nf,df->nd", grad_up_pre, up_w, preferred_element_type=f32)
+        + jnp.einsum("ne,de->nd", grad_logits, full_router, preferred_element_type=f32)
+    ).astype(bf16)
+    grad_normed = scatter_all(grad_normed_part[:half_rows], grad_normed_part[half_rows:])
+
+    def transposed(left_op, right_op):
+        return jnp.einsum("nd,nf->df", left_op, right_op, preferred_element_type=f32)
+
+    def give_back(gradient):
+        gradient = gradient.astype(bf16).reshape(8, 256, mine, hidden_units)
+        gradient = exchange(jnp.transpose(gradient, (0, 2, 1, 3)))
+        return gradient.reshape(experts, 256, hidden_units).astype(f32)
+
+    grad_down_w = give_back(transposed(dm, hidden))
+    grad_gate_w = give_back(transposed(nf, grad_gate_pre))
+    grad_up_w = give_back(transposed(nf, grad_up_pre))
+    grad_router_part = transposed(nf, grad_logits)
+
+    upstream = own_cot.astype(f32)
+    grad_ffn_part = jnp.sum(grad_normed * unit_two, axis=(0, 1))
+    grad_middle = upstream + norm_back(grad_normed, middle, scale_two, ffn_vec)
+
+    grad_branch = gather_heads(grad_middle.astype(bf16))
+    grad_att = product(grad_branch, w_o)
+    grad_out_part = jnp.einsum("snd,snc->dc", grad_branch, attended_low, preferred_element_type=f32)
+    grad_acc = (grad_att / denominator).astype(bf16)
+    grad_total = -jnp.sum(grad_att * attended, axis=-1, keepdims=True) / denominator
+    grad_prob = jnp.einsum("sqd,skd->sqk", grad_acc, value_rows, preferred_element_type=f32)
+    grad_score = (exponent * (grad_prob + grad_total)).astype(bf16)
+    grad_query = jnp.einsum("sqk,skd->sqd", grad_score, keys, preferred_element_type=f32)
+    grad_keys = jnp.einsum("sqk,sqd->skd", grad_score, query, preferred_element_type=f32)
+    grad_values = jnp.einsum("sqk,sqd->skd", expo_low, grad_acc, preferred_element_type=f32)
+    query_norm_grad = rotate(grad_query * score_scale, cosines, -sines)
+    key_norm_grad = rotate(grad_keys, cosines, -sines)
+    grad_qk_part = jnp.stack(
+        [jnp.sum(query_norm_grad * query_hat, axis=(0, 1)), jnp.sum(key_norm_grad * key_hat, axis=(0, 1))], axis=1
+    )
+    grad_lin = jnp.concatenate(
+        [
+            norm_back(query_norm_grad, query_lin, query_scale, query_gain).astype(bf16),
+            norm_back(key_norm_grad, key_lin, key_scale, key_gain).astype(bf16),
+            grad_values.astype(bf16),
+        ],
+        axis=-1,
+    )
+    grad_normed_attn = jnp.einsum("snc,dc->snd", grad_lin, w_qkv, preferred_element_type=f32)
+    grad_attn_part = jnp.sum(grad_normed_attn * unit, axis=(0, 1))
+    grad_normed_one = scatter_heads(grad_normed_attn.astype(bf16))
+    own_inputs = own_tokens.astype(f32)
+    grad_inputs = grad_middle + norm_back(grad_normed_one, own_inputs, inverse_rms(own_inputs), attn_vec)
+
+    grad_qkv_part = jnp.einsum("snd,snc->dc", normed, grad_lin, preferred_element_type=f32)
+    dense_grad = jnp.concatenate([grad_qkv_part, grad_out_part], axis=1).astype(bf16).reshape(8, 256, 4, head_size)
+    dense_grad = exchange(dense_grad).astype(f32).reshape(4, 2, 256, 4, head_size).sum(1)
+    dense_grad = jnp.transpose(dense_grad, (2, 1, 0, 3)).reshape(4, 256, 4 * head_size)
+
+    small = jnp.zeros((width, 20), f32)
+    small = small.at[:, :16].set(grad_router_part).at[:, 16].set(grad_attn_part).at[:, 17].set(grad_ffn_part)
+    small = small.reshape(8, 256, 20).at[:, :16, 18:20].set(grad_qk_part.reshape(8, 16, 2)).reshape(width, 20)
+    small = lax.psum(lax.psum_scatter(small, "ctx", scatter_dimension=0, tiled=True), "tp")
+
+    def hand_out(owned):
+        kept, received = owned[:, :16], xor_permute(owned[:, 16:], BIT_X)
+        rows = jnp.where(x == 0, jnp.concatenate([kept, received], 0), jnp.concatenate([received, kept], 0))
+        return lax.all_gather(rows, "tp", axis=1, tiled=True)
+
+    return (
+        hand_out(layer_out),
+        hand_out(grad_inputs.astype(bf16)),
+        small[:, 16],
+        small[:, 17],
+        small[:16, 18:20],
+        dense_grad[0],
+        dense_grad[1],
+        dense_grad[2],
+        dense_grad[3],
+        small[:, :16],
+        grad_gate_w,
+        grad_up_w,
+        grad_down_w,
+    )
+
+
 def solution(mesh):
+    fast = mesh.shape["ctx"] == 8 and mesh.shape["tp"] == 4
     return jax.shard_map(
-        per_device,
+        per_device_fast if fast else per_device,
         mesh=mesh,
         in_specs=(
             P(None, "ctx", None),

time: 2960 us -> 1060 us (0.36)
  waiting for transfers between devices: 2250 us -> 449 us
  matrix products: 320 us -> 119 us
  starting transfers between devices: 2.78 us -> 160 us
  other arithmetic: 155 us -> 67.2 us
  local copies, waits for them, and re-layouts: 99.1 us -> 161 us
    reduce_scatter x12 -> x1, waiting for transfers between devices: 1250 us -> 55.4 us  [per_device_fast(): lax.psum_scatter(small, 'ctx', scatter_dimension=0, tiled=True)]
    all_gather x11 -> x2, waiting for transfers between devices: 908 us -> 0.01 us  [hand_out(): return lax.all_gather(rows, 'tp', axis=1, tiled=True)]
    ppermute x0 -> x72, waiting for transfers between devices: none -> 353 us  [xor_permute(): lax.ppermute(array, ('ctx', 'tp'), [(i, i ^ mask) for i in range(32)])]
    dot_general x52 -> x18, matrix products: 306 us -> 85 us  [the longest x4 34.1 us: transposed(): jnp.einsum('nd,nf->df', left_op, right_op, preferred_element_type=f32)]
    ppermute x0 -> x72, starting transfers between devices: none -> 110 us  [xor_permute(): lax.ppermute(array, ('ctx', 'tp'), [(i, i ^ mask) for i in range(32)])]
    scatter-add x4 -> x0, other arithmetic: 87.2 us -> none  [the longest x2 43.9 us: per_device(): grad_normed_part = jnp.zeros((row_count, model_width), jnp.float32).at[so...]
    psum x3 -> x0, waiting for transfers between devices: 81.2 us -> none  [the longest x1 50.4 us: per_device(): lax.psum(grad_normed_part, 'tp')]
    unnamed x287 -> x253, local copies, waits for them, and re-layouts: 11.2 us -> 73.4 us
  transfers between devices with their start and end apart: 27 -> 83, of which waited for: 23 -> 36; matrix products, arithmetic and copies ran while one was open for 13% -> 26% of each run, Pallas kernels for 0% -> 0%
where the time goes in v1:
time: 1060 us; the launch traced here: 1050 us
  waiting for transfers between devices  449 us (42%)
  local copies, waits for them, and re-layouts  161 us (15%)
  starting transfers between devices  160 us (15%)
  matrix products  119 us (11%)
  blocking collectives  79.8 us (8%)
  other arithmetic  67.2 us (6%)
  between operations  17.7 us (2%)
    ppermute x72, waiting for transfers between devices, xor_permute(): lax.ppermute(array, ('ctx', 'tp'), [(i, i ^ mask) for i in range(32)])  353 us
    ppermute x72, starting transfers between devices, xor_permute(): lax.ppermute(array, ('ctx', 'tp'), [(i, i ^ mask) for i in range(32)])  110 us
    unnamed x253, local copies, waits for them, and re-layouts  73.4 us
    reduce_scatter x1, waiting for transfers between devices, per_device_fast(): lax.psum_scatter(small, 'ctx', scatter_dimension=0, tiled=True)  55.4 us
    all_to_all x8, starting transfers between devices, exchange(): return lax.all_to_all(array, 'ctx', 0, 0, tiled=True)  49.9 us
    all_gather x1, blocking collectives, per_device_fast(): pack = lax.all_gather(pack, 'ctx', axis=0, tiled=True)  41.7 us
    all_to_all x8, waiting for transfers between devices, exchange(): return lax.all_to_all(array, 'ctx', 0, 0, tiled=True)  41 us
    dot_general x4, matrix products, transposed(): jnp.einsum('nd,nf->df', left_op, right_op, preferred_element_type=f32)  34.1 us
  transfers between devices with their start and end apart: 83, of which 36 were waited for; matrix products, arithmetic and copies ran while one was open for 26% of the time, Pallas kernels for 0%

profile of v1, /device:TPU:29, one launch (start us, length us, event | category | flops | bytes accessed | tf_op | source)
XLA Modules:
  0.0 1053.5 jit_solution(16352162622782460340)
XLA Ops:
  22.8 12.5 %collective-permute-done.2 = bf16[2,32,2048]{2,1,0:T(8,128)(2,1)S(1)} collective-permute-done((bf16[2,32,2048]{2,1,0:T(8,128)(2,1)S(1)}, bf16[2,32,2048]{2,1,0:T(8,128)(2,1)S(1)}, u32[]{:S(2)}, u32[]{:S(2)}) %collective-permute-start.2) | collective-permute-done | bytes 262176 | tf_op jit(solution)/shard_map/ppermute | solution.py:454
  68.4 41.7 %all_gather.12 = bf16[2048,20]{0,1:T(8,128)(2,1)S(1)} all-gather(bf16[256,20]{0,1:T(8,128)(2,1)S(1)} %scatter.31), channel_id=1, replica_groups=mesh['ctx'=8,'tp'=4] {'ctx'}, dimensions={0}, use_global_device_ids=true | all-gather | bytes 92160 | tf_op jit(solution)/shard_map/all_gather | solution.py:530
  162.9 9.7 collective-permute-done.40
  189.6 9.9 collective-permute-done.41
  203.8 19.6 %collective-permute-done.8 = bf16[2,32,2048]{2,1,0:T(8,128)(2,1)S(1)} collective-permute-done((bf16[2,32,2048]{2,1,0:T(8,128)(2,1)S(1)}, bf16[2,32,2048]{2,1,0:T(8,128)(2,1)S(1)}, u32[]{:S(2)}, u32[]{:S(2)}) %collective-permute-start.8) | collective-permute-done | bytes 262176 | tf_op jit(solution)/shard_map/ppermute | solution.py:454
  230.3 24.4 %collective-permute-done.9 = bf16[2,32,2048]{2,1,0:T(8,128)(2,1)S(1)} collective-permute-done((bf16[2,32,2048]{2,1,0:T(8,128)(2,1)S(1)}, bf16[2,32,2048]{2,1,0:T(8,128)(2,1)S(1)}, u32[]{:S(2)}, u32[]{:S(2)}) %collective-permute-start.9) | collective-permute-done | bytes 262176 | tf_op jit(solution)/shard_map/ppermute | solution.py:454
  291.8 14.8 %collective-permute-done.15 = bf16[256,2048]{1,0:T(8,128)(2,1)} collective-permute-done((bf16[256,2048]{1,0:T(8,128)(2,1)}, bf16[256,2048]{1,0:T(8,128)(2,1)}, u32[]{:S(2)}, u32[]{:S(2)}) %collective-permute-start.15) | collective-permute-done | bytes 1048608 | tf_op jit(solution)/shard_map/ppermute | solution.py:454
  327.5 22.3 %collective-permute-done.44 = bf16[32,2048]{1,0:T(8,128)(2,1)} collective-permute-done((bf16[32,2048]{1,0:T(8,128)(2,1)S(1)}, bf16[32,2048]{1,0:T(8,128)(2,1)}, u32[]{:S(2)}, u32[]{:S(2)}) %collective-permute-start.44) | collective-permute-done | bytes 131104 | tf_op jit(solution)/shard_map/ppermute | solution.py:454
  393.7 12.2 %collective-permute-start.48 = (bf16[512,2048]{1,0:T(8,128)(2,1)}, bf16[512,2048]{1,0:T(8,128)(2,1)}, u32[]{:S(2)}, u32[]{:S(2)}) collective-permute-start(bf16[512,2048]{1,0:T(8,128)(2,1)} %get-tuple-element.215), channel_id=1, source_target_pairs={{0,1},{1,0},{2,3},{3,2},{4,5},{5,4},{6,7},{7,6},{8,9},{9,8},{10,11... | collective-permute-start | bytes 6291464 | tf_op jit(solution)/shard_map/ppermute | solution.py:454
  405.9 28.7 %collective-permute-done.21 = bf16[256,2048]{1,0:T(8,128)(2,1)S(1)} collective-permute-done((bf16[256,2048]{1,0:T(8,128)(2,1)}, bf16[256,2048]{1,0:T(8,128)(2,1)S(1)}, u32[]{:S(2)}, u32[]{:S(2)}) %collective-permute-start.21) | collective-permute-done | bytes 1048608 | tf_op jit(solution)/shard_map/ppermute | solution.py:454
  437.8 25.2 %all_gather.13 = s32[4,512,8]{2,0,1:T(4,128)S(1)} all-gather(s32[4,64,8]{2,0,1:T(4,128)S(1)} %copy.218), channel_id=1, replica_groups=mesh['ctx'=8,'tp'=4] {'ctx'}, dimensions={1}, use_global_device_ids=true | all-gather | bytes 73728 | tf_op jit(solution)/shard_map/all_gather | solution.py:535
  547.0 15.3 %add_convert_fusion = bf16[2048,2048]{1,0:T(8,128)(2,1)} fusion(f32[2048,2048]{1,0:T(8,128)} %fusion.69, f32[2048,2048]{1,0:T(8,128)} %fusion.70, bf16[2048,16]{0,1:T(8,128)(2,1)S(1)} %multiply_convert_fusion.4, bf16[2048,20]{0,1:T(8,128)(2,1)S(1)} %all_gather.12), kind=kOutput, calls=%fused_computation.1 | convolution fusion | flops 146800640 | bytes 42074112 | tf_op jit(solution)/shard_map/ne,de->nd/dot_general | solution.py:640
  580.9 19.0 %collective-permute-done.30 = bf16[256,2048]{1,0:T(8,128)(2,1)S(1)} collective-permute-done((bf16[256,2048]{1,0:T(8,128)(2,1)}, bf16[256,2048]{1,0:T(8,128)(2,1)S(1)}, u32[]{:S(2)}, u32[]{:S(2)}) %collective-permute-start.30) | collective-permute-done | bytes 1048608 | tf_op jit(solution)/shard_map/ppermute | solution.py:454
  603.3 19.1 %collective-permute-done.56 = bf16[256,2048]{1,0:T(8,128)(2,1)S(1)} collective-permute-done((bf16[256,2048]{1,0:T(8,128)(2,1)S(1)}, bf16[256,2048]{1,0:T(8,128)(2,1)S(1)}, u32[]{:S(2)}, u32[]{:S(2)}) %collective-permute-start.56) | collective-permute-done | bytes 1048608 | tf_op jit(solution)/shard_map/ppermute | solution.py:454
  664.9 12.0 %collective-permute-done.59 = bf16[32,2048]{1,0:T(8,128)(2,1)S(1)} collective-permute-done((bf16[32,2048]{1,0:T(8,128)(2,1)S(1)}, bf16[32,2048]{1,0:T(8,128)(2,1)S(1)}, u32[]{:S(2)}, u32[]{:S(2)}) %collective-permute-start.59) | collective-permute-done | bytes 131104 | tf_op jit(solution)/shard_map/ppermute | solution.py:454
  693.3 12.8 %collective-permute-done.62 = bf16[2,32,2048]{2,1,0:T(8,128)(2,1)S(1)} collective-permute-done((bf16[2,32,2048]{2,1,0:T(8,128)(2,1)S(1)}, bf16[2,32,2048]{2,1,0:T(8,128)(2,1)S(1)}, u32[]{:S(2)}, u32[]{:S(2)}) %collective-permute-start.62) | collective-permute-done | bytes 262176 | tf_op jit(solution)/shard_map/ppermute | solution.py:454
  711.5 17.2 %collective-permute-done.64 = bf16[2,128,2048]{2,1,0:T(8,128)(2,1)S(1)} collective-permute-done((bf16[2,128,2048]{2,1,0:T(8,128)(2,1)S(1)}, bf16[2,128,2048]{2,1,0:T(8,128)(2,1)S(1)}, u32[]{:S(2)}, u32[]{:S(2)}) %collective-permute-start.64) | collective-permute-done | bytes 1048608 | tf_op jit(solution)/shard_map/ppermute | solution.py:454
  733.4 9.7 convolution_convert_fusion.2
  779.7 21.9 %all-to-all-done.7 = bf16[8,2,256,256]{3,2,1,0:T(8,128)(2,1)} async-done(((bf16[8,2,256,256]{3,2,1,0:T(8,128)(2,1)}), bf16[8,2,256,256]{3,2,1,0:T(8,128)(2,1)}, u32[]{:S(2)}, u32[]{:S(2)}) %all-to-all-start.7) | async-done | bytes 2097184 | tf_op jit(solution)/shard_map/all_to_all | solution.py:511
  835.2 19.1 %all-to-all-done.6 = bf16[8,2,256,256]{3,2,1,0:T(8,128)(2,1)} async-done(((bf16[8,2,256,256]{3,2,1,0:T(8,128)(2,1)}), bf16[8,2,256,256]{3,2,1,0:T(8,128)(2,1)}, u32[]{:S(2)}, u32[]{:S(2)}) %all-to-all-start.6) | async-done | bytes 2097184 | tf_op jit(solution)/shard_map/all_to_all | solution.py:511
  881.1 21.8 %collective-permute-done.67 = bf16[2,128,2048]{2,1,0:T(8,128)(2,1)} collective-permute-done((bf16[2,128,2048]{2,1,0:T(8,128)(2,1)}, bf16[2,128,2048]{2,1,0:T(8,128)(2,1)}, u32[]{:S(2)}, u32[]{:S(2)}) %collective-permute-start.67) | collective-permute-done | bytes 1048608 | tf_op jit(solution)/shard_map/ppermute | solution.py:454
  921.7 15.4 %collective-permute-done.69 = bf16[2,32,2048]{2,1,0:T(8,128)(2,1)} collective-permute-done((bf16[2,32,2048]{2,1,0:T(8,128)(2,1)}, bf16[2,32,2048]{2,1,0:T(8,128)(2,1)}, u32[]{:S(2)}, u32[]{:S(2)}) %collective-permute-start.69) | collective-permute-done | bytes 262176 | tf_op jit(solution)/shard_map/ppermute | solution.py:454
  966.6 55.4 %reduce-scatter.2.cloned.1.call-done = f32[256,20]{0,1:T(8,128)} async-done(((f32[2048,20]{0,1:T(8,128)}), f32[256,20]{0,1:T(8,128)}) %reduce-scatter.2.cloned.1.call-update) | async-done | bytes 20496 | tf_op jit(solution)/shard_map/reduce_scatter | solution.py:698
  1022.0 13.0 %psum.7 = f32[256,20]{0,1:T(8,128)S(1)} all-reduce(f32[256,20]{0,1:T(8,128)} %reduce-scatter.2.cloned.1.call-done), channel_id=1, replica_groups=mesh['ctx'=8,'tp'=4] {'tp'}, use_global_device_ids=true, to_apply=%region_27.28 | all-reduce | flops 5120 | bytes 40960 | tf_op jit(solution)/shard_map/psum | solution.py:698
  (606 shorter events, 563.4 us)
Async XLA Ops:
  40.5 75.5 %all-to-all-start = ((bf16[8,256,4,128]{3,1,2,0:T(8,128)(2,1)}), bf16[8,256,4,128]{3,1,2,0:T(8,128)(2,1)}, u32[]{:S(2)}, u32[]{:S(2)}) async-start(bf16[8,256,4,128]{3,1,2,0:T(8,128)(2,1)} %bitcast.4), calls=%async_computation | async-start | bytes 4194304 | tf_op jit(solution)/shard_map/all_to_all | solution.py:511
  59.9 51.6 %collective-permute-start.5 = (bf16[2,256,2048]{2,1,0:T(8,128)(2,1)}, bf16[2,256,2048]{2,1,0:T(8,128)(2,1)S(1)}, u32[]{:S(2)}, u32[]{:S(2)}) collective-permute-start(bf16[2,256,2048]{2,1,0:T(8,128)(2,1)} %get-tuple-element.224), channel_id=1, source_target_pairs={{0,1},{1,0},{2,3},{3,2},{4,5},{5,4},{6,7},{7,6},{8,9},{9,8},{10,11... | collective-permute-start | bytes 6291464 | tf_op jit(solution)/shard_map/ppermute | solution.py:454
  179.0 106.6 %all-to-all-start.1 = ((bf16[8,2,256,256]{2,3,1,0:T(8,128)(2,1)}), bf16[8,2,256,256]{2,3,1,0:T(8,128)(2,1)}, u32[]{:S(2)}, u32[]{:S(2)}) async-start(bf16[8,2,256,256]{2,3,1,0:T(8,128)(2,1)} %bitcast.188), calls=%async_computation.1 | async-start | bytes 4194304 | tf_op jit(solution)/shard_map/all_to_all | solution.py:511
  187.2 43.1 %collective-permute-start.10 = (bf16[2,32,2048]{2,1,0:T(8,128)(2,1)S(1)}, bf16[2,32,2048]{2,1,0:T(8,128)(2,1)S(1)}, u32[]{:S(2)}, u32[]{:S(2)}) collective-permute-start(bf16[2,32,2048]{2,1,0:T(8,128)(2,1)S(1)} %get-tuple-element.222), channel_id=1, source_target_pairs={{0,24},{1,25},{2,26},{3,27},{4,28},{5,29},{6,30},{7,31},{8,16},{9,... | collective-permute-start | bytes 786440 | tf_op jit(solution)/shard_map/ppermute | solution.py:454
  188.4 66.4 %collective-permute-start.9 = (bf16[2,32,2048]{2,1,0:T(8,128)(2,1)S(1)}, bf16[2,32,2048]{2,1,0:T(8,128)(2,1)S(1)}, u32[]{:S(2)}, u32[]{:S(2)}) collective-permute-start(bf16[2,32,2048]{2,1,0:T(8,128)(2,1)S(1)} %get-tuple-element.223), channel_id=1, source_target_pairs={{0,16},{1,17},{2,18},{3,19},{4,20},{5,21},{6,22},{7,23},{8,24},{9,... | collective-permute-start | bytes 786440 | tf_op jit(solution)/shard_map/ppermute | solution.py:454
  202.3 149.7 %collective-permute-start.42 = (bf16[512,2048]{1,0:T(8,128)(2,1)}, bf16[512,2048]{1,0:T(8,128)(2,1)}, u32[]{:S(2)}, u32[]{:S(2)}) collective-permute-start(bf16[512,2048]{1,0:T(8,128)(2,1)} %get-tuple-element.217), channel_id=1, source_target_pairs={{0,1},{1,0},{2,3},{3,2},{4,5},{5,4},{6,7},{7,6},{8,9},{9,8},{10,11... | collective-permute-start | bytes 6291464 | tf_op jit(solution)/shard_map/ppermute | solution.py:454
  285.6 93.8 %all-to-all-start.2 = ((bf16[8,2,256,256]{2,3,1,0:T(8,128)(2,1)}), bf16[8,2,256,256]{2,3,1,0:T(8,128)(2,1)S(1)}, u32[]{:S(2)}, u32[]{:S(2)}) async-start(bf16[8,2,256,256]{2,3,1,0:T(8,128)(2,1)} %bitcast.187), calls=%async_computation.2 | async-start | bytes 4194304 | tf_op jit(solution)/shard_map/all_to_all | solution.py:511
  309.3 63.8 %collective-permute-start.16 = (bf16[512,2048]{1,0:T(8,128)(2,1)}, bf16[512,2048]{1,0:T(8,128)(2,1)}, u32[]{:S(2)}, u32[]{:S(2)}) collective-permute-start(bf16[512,2048]{1,0:T(8,128)(2,1)} %get-tuple-element.213), channel_id=1, source_target_pairs={{0,1},{1,0},{2,3},{3,2},{4,5},{5,4},{6,7},{7,6},{8,9},{9,8},{10,11... | collective-permute-start | bytes 6291464 | tf_op jit(solution)/shard_map/ppermute | solution.py:454
  312.2 37.6 %collective-permute-start.43 = (bf16[32,2048]{1,0:T(8,128)(2,1)S(1)}, bf16[32,2048]{1,0:T(8,128)(2,1)}, u32[]{:S(2)}, u32[]{:S(2)}) collective-permute-start(bf16[32,2048]{1,0:T(8,128)(2,1)S(1)} %get-tuple-element.178), channel_id=1, source_target_pairs={{0,8},{1,9},{2,10},{3,11},{4,12},{5,13},{6,14},{7,15},{8,0},{9,1},... | collective-permute-start | bytes 393224 | tf_op jit(solution)/shard_map/ppermute | solution.py:454
  380.7 96.3 %all-to-all-start.3 = ((bf16[8,2,256,256]{2,3,1,0:T(8,128)(2,1)}), bf16[8,2,256,256]{2,3,1,0:T(8,128)(2,1)}, u32[]{:S(2)}, u32[]{:S(2)}) async-start(bf16[8,2,256,256]{2,3,1,0:T(8,128)(2,1)} %bitcast.186), calls=%async_computation.3 | async-start | bytes 4194304 | tf_op jit(solution)/shard_map/all_to_all | solution.py:511
  389.3 45.3 %collective-permute-start.21 = (bf16[256,2048]{1,0:T(8,128)(2,1)}, bf16[256,2048]{1,0:T(8,128)(2,1)S(1)}, u32[]{:S(2)}, u32[]{:S(2)}) collective-permute-start(bf16[256,2048]{1,0:T(8,128)(2,1)} %get-tuple-element.250), channel_id=1, source_target_pairs={{0,4},{1,5},{2,6},{3,7},{4,0},{5,1},{6,2},{7,3},{8,12},{9,13},{10,... | collective-permute-start | bytes 3145736 | tf_op jit(solution)/shard_map/ppermute | solution.py:454
  393.7 86.8 %collective-permute-start.48 = (bf16[512,2048]{1,0:T(8,128)(2,1)}, bf16[512,2048]{1,0:T(8,128)(2,1)}, u32[]{:S(2)}, u32[]{:S(2)}) collective-permute-start(bf16[512,2048]{1,0:T(8,128)(2,1)} %get-tuple-element.215), channel_id=1, source_target_pairs={{0,1},{1,0},{2,3},{3,2},{4,5},{5,4},{6,7},{7,6},{8,9},{9,8},{10,11... | collective-permute-start | bytes 6291464 | tf_op jit(solution)/shard_map/ppermute | solution.py:454
  436.1 47.5 %collective-permute-start.22 = (bf16[512,2048]{1,0:T(8,128)(2,1)}, bf16[512,2048]{1,0:T(8,128)(2,1)}, u32[]{:S(2)}, u32[]{:S(2)}) collective-permute-start(bf16[512,2048]{1,0:T(8,128)(2,1)} %get-tuple-element.211), channel_id=1, source_target_pairs={{0,1},{1,0},{2,3},{3,2},{4,5},{5,4},{6,7},{7,6},{8,9},{9,8},{10,11... | collective-permute-start | bytes 6291464 | tf_op jit(solution)/shard_map/ppermute | solution.py:454
  525.2 40.6 %collective-permute-start.23 = (bf16[512,2048]{1,0:T(8,128)(2,1)}, bf16[512,2048]{1,0:T(8,128)(2,1)}, u32[]{:S(2)}, u32[]{:S(2)}) collective-permute-start(bf16[512,2048]{1,0:T(8,128)(2,1)} %get-tuple-element.196), channel_id=1, source_target_pairs={{0,1},{1,0},{2,3},{3,2},{4,5},{5,4},{6,7},{7,6},{8,9},{9,8},{10,11... | collective-permute-start | bytes 6291464 | tf_op jit(solution)/shard_map/ppermute | solution.py:454
  580.5 41.8 %collective-permute-start.56 = (bf16[256,2048]{1,0:T(8,128)(2,1)S(1)}, bf16[256,2048]{1,0:T(8,128)(2,1)S(1)}, u32[]{:S(2)}, u32[]{:S(2)}) collective-permute-start(bf16[256,2048]{1,0:T(8,128)(2,1)S(1)} %slice.600), channel_id=1, source_target_pairs={{0,4},{1,5},{2,6},{3,7},{4,0},{5,1},{6,2},{7,3},{8,12},{9,13},{10,... | collective-permute-start | bytes 3145736 | tf_op jit(solution)/shard_map/ppermute | solution.py:454
  580.6 43.5 %collective-permute-start.50 = (bf16[256,2048]{1,0:T(8,128)(2,1)S(1)}, bf16[256,2048]{1,0:T(8,128)(2,1)S(1)}, u32[]{:S(2)}, u32[]{:S(2)}) collective-permute-start(bf16[256,2048]{1,0:T(8,128)(2,1)S(1)} %slice.590), channel_id=1, source_target_pairs={{0,2},{1,3},{2,0},{3,1},{4,6},{5,7},{6,4},{7,5},{8,10},{9,11},{10,... | collective-permute-start | bytes 3145736 | tf_op jit(solution)/shard_map/ppermute | solution.py:454
  747.4 54.3 %all-to-all-start.7 = ((bf16[8,2,256,256]{3,2,1,0:T(8,128)(2,1)}), bf16[8,2,256,256]{3,2,1,0:T(8,128)(2,1)}, u32[]{:S(2)}, u32[]{:S(2)}) async-start(bf16[8,2,256,256]{3,2,1,0:T(8,128)(2,1)} %bitcast.176), calls=%async_computation.8 | async-start | bytes 4194304 | tf_op jit(solution)/shard_map/all_to_all | solution.py:511
  801.6 52.7 %all-to-all-start.6 = ((bf16[8,2,256,256]{3,2,1,0:T(8,128)(2,1)}), bf16[8,2,256,256]{3,2,1,0:T(8,128)(2,1)}, u32[]{:S(2)}, u32[]{:S(2)}) async-start(bf16[8,2,256,256]{3,2,1,0:T(8,128)(2,1)} %bitcast.189), calls=%async_computation.7 | async-start | bytes 4194304 | tf_op jit(solution)/shard_map/all_to_all | solution.py:511
  818.9 50.2 %collective-permute-start.66 = (bf16[2,256,2048]{2,1,0:T(8,128)(2,1)}, bf16[2,256,2048]{2,1,0:T(8,128)(2,1)}, u32[]{:S(2)}, u32[]{:S(2)}) collective-permute-start(bf16[2,256,2048]{2,1,0:T(8,128)(2,1)} %slice.612), channel_id=1, source_target_pairs={{0,1},{1,0},{2,3},{3,2},{4,5},{5,4},{6,7},{7,6},{8,9},{9,8},{10,11... | collective-permute-start | bytes 6291464 | tf_op jit(solution)/shard_map/ppermute | solution.py:454
  854.3 54.7 %all-to-all-start.5 = ((bf16[8,2,256,256]{3,2,1,0:T(8,128)(2,1)}), bf16[8,2,256,256]{3,2,1,0:T(8,128)(2,1)}, u32[]{:S(2)}, u32[]{:S(2)}) async-start(bf16[8,2,256,256]{3,2,1,0:T(8,128)(2,1)} %bitcast.178), calls=%async_computation.6 | async-start | bytes 4194304 | tf_op jit(solution)/shard_map/all_to_all | solution.py:511
  859.0 107.6 %all-gather.3.cloned.1.call-start = ((), (), s32[]{:S(2)}) async-start(), calls=%async_computation.9 | async-start | bytes 1310720 | tf_op jit(solution)/shard_map/all_gather | solution.py:703
  909.0 127.7 %all-to-all-start.4 = ((bf16[8,256,4,128]{1,3,2,0:T(8,128)(2,1)}), bf16[8,256,4,128]{1,3,2,0:T(8,128)(2,1)S(1)}, u32[]{:S(2)}, u32[]{:S(2)}) async-start(bf16[8,256,4,128]{1,3,2,0:T(8,128)(2,1)} %copy.236), calls=%async_computation.5 | async-start | bytes 4194304 | tf_op jit(solution)/shard_map/all_to_all | solution.py:511
  914.5 107.5 %reduce-scatter.2.cloned.1.call-start = ((), (), s32[]{:S(2)}) async-start(), calls=%async_computation.11 | async-start | bytes 221184 | tf_op jit(solution)/shard_map/reduce_scatter | solution.py:698
  953.6 89.6 %all-gather.5.cloned.1.call-start = ((), (), s32[]{:S(2)}) async-start(), calls=%async_computation.10 | async-start | bytes 1310720 | tf_op jit(solution)/shard_map/all_gather | solution.py:703
  (159 other events, 3267.9 us)
Sparse Core Ops, SparseCore 0:
  866.1 23.5 all-gather.2
  956.6 25.9 all-gather.4
Sparse Core Ops, SparseCore 1:
  953.7 68.2 reduce-scatter.1

commit v2 on v0

--- a/solution.py
+++ b/solution.py
@@ -1,6 +1,9 @@
 import jax
 import jax.numpy as jnp
+import numpy as np
 from jax import lax
+from jax.experimental import pallas as pl
+from jax.experimental.pallas import tpu as pltpu
 from jax.sharding import PartitionSpec as P
 
 MICRO = 2
@@ -450,9 +453,1182 @@
     return (layer_out, input_grad) + tuple(dense_owned) + tuple(expert_owned)
 
 
+MESH_ID = pl.DeviceIdType.MESH
+F32, BF16 = jnp.float32, jnp.bfloat16
+VMEM_LIMIT = 63 * 1024 * 1024
+
+
+class Place:
+    def __init__(self, z, x, y, k):
+        self.z, self.x, self.y, self.k = z, x, y, k
+        self.ctx, self.tp = z * 2 + x, y * 2 + k
+        self.owner32 = self.ctx * 4 + self.tp
+        self.owner16 = z * 4 + self.tp
+        self.owner8 = x * 4 + self.tp
+        self.device = (self.ctx, self.tp)
+
+    def flip(self, dims):
+        z, x, y, k = self.z, self.x, self.y, self.k
+        for dim in dims:
+            if dim == "Z":
+                z = z + 2 - 4 * (z // 2)
+            elif dim == "z":
+                z = z + 1 - 2 * (z % 2)
+            elif dim == "x":
+                x = 1 - x
+            elif dim == "y":
+                y = 1 - y
+            else:
+                k = 1 - k
+        return Place(z, x, y, k)
+
+
+def my_place():
+    ctx, tp = lax.axis_index("ctx"), lax.axis_index("tp")
+    return Place(ctx // 2, ctx % 2, tp // 2, tp % 2)
+
+
+def ctx_peer(here, step):
+    ctx = (here.ctx + step) % 8
+    return Place(ctx // 2, ctx % 2, here.y, here.k)
+
+
+def everyone(here):
+    return [ctx_peer(here, step) for step in range(1, 8)] + [here.flip("y"), here.flip("k")]
+
+
+def greet(here):
+    barrier = pltpu.get_barrier_semaphore()
+    peers = everyone(here)
+    for peer in peers:
+        pl.semaphore_signal(barrier, inc=1, device_id=peer.device, device_id_type=MESH_ID)
+    pl.semaphore_wait(barrier, len(peers))
+
+
+def remote(source, target, send_sem, recv_sem, peer):
+    return pltpu.make_async_remote_copy(
+        src_ref=source,
+        dst_ref=target,
+        send_sem=send_sem,
+        recv_sem=recv_sem,
+        device_id=peer.device,
+        device_id_type=MESH_ID,
+    )
+
+
+def subsets(dims):
+    found = [""]
+    for dim in dims:
+        found = found + [one + dim for one in found]
+    return sorted(found, key=len)
+
+
+class Gather:
+    def __init__(self, here, dims, slot, send_sems, recv_sems, own=None):
+        self.here, self.dims, self.slot, self.own = here, dims, slot, own
+        self.send_sems, self.recv_sems = send_sems, recv_sems
+        self.started = []
+
+    def number(self, r):
+        return sum(1 << self.dims.index(dim) for dim in r)
+
+    def copy(self, r, dim):
+        block = self.slot(self.here.flip(r))
+        source = self.own if (r == "" and self.own is not None) else block
+        i = self.number(r + dim)
+        return remote(source, block, self.send_sems.at[i], self.recv_sems.at[i], self.here.flip(dim))
+
+    def send(self, r):
+        last = max([self.dims.index(dim) for dim in r], default=-1)
+        for dim in self.dims[last + 1 :]:
+            copy = self.copy(r, dim)
+            copy.start()
+            self.started.append(copy)
+
+    def arrive(self, r):
+        block = self.slot(self.here.flip(r))
+        i = self.number(r)
+        last = self.dims[max(self.dims.index(dim) for dim in r)]
+        remote(block, block, self.send_sems.at[i], self.recv_sems.at[i], self.here.flip(last)).wait_recv()
+        self.send(r)
+
+    def sort(self, r):
+        return "".join(dim for dim in self.dims if dim in r)
+
+    def order(self):
+        inner = [r for r in subsets(self.dims) if r and self.dims[-1] not in r]
+        outer = [r for r in subsets(self.dims) if self.dims[-1] in r]
+        return inner + outer
+
+    def finish(self):
+        for copy in self.started:
+            copy.wait_send()
+
+
+def add_blocks(target, left, right, extra=None):
+    rows = left.shape[0]
+
+    def one(i, carry):
+        part = pl.ds(pl.multiple_of(i * 16, 16), 16)
+        total = left[part, :].astype(F32) + right[part, :].astype(F32)
+        target[part, :] = total.astype(target.dtype)
+        return carry
+
+    lax.fori_loop(0, rows // 16, one, 0)
+
+
+class Scatter:
+    def __init__(self, here, dims, first, slot, received, send_sems, recv_sems):
+        self.here, self.dims, self.first, self.slot, self.received = here, dims, first, slot, received
+        self.send_sems, self.recv_sems = send_sems, recv_sems
+        self.started = []
+
+    def number(self, level, r):
+        return sum(1 << self.dims[level + 1 :].index(dim) for dim in r)
+
+    def sem(self, level, r):
+        below = sum(1 << (len(self.dims) - 1 - i) for i in range(level))
+        return below + self.number(level, r)
+
+    def copy(self, level, r):
+        dim = self.dims[level]
+        source = self.first(self.here.flip(r + dim)) if level == 0 else self.slot(r + dim)
+        i = self.sem(level, r)
+        return remote(
+            source, self.received(level, self.number(level, r)), self.send_sems.at[i], self.recv_sems.at[i], self.here.flip(dim)
+        )
+
+    def ordered(self, level):
+        rest = self.dims[level + 1 :]
+        return sorted(subsets(rest), key=lambda r: [-(dim in r) for dim in rest])
+
+    def send(self, level, r):
+        copy = self.copy(level, r)
+        copy.start()
+        self.started.append(copy)
+
+    def start(self):
+        for r in self.ordered(0):
+            self.send(0, r)
+
+    def take(self, level, r):
+        self.copy(level, r).wait_recv()
+        add_blocks(self.slot(r), self.slot(r), self.received(level, self.number(level, r)))
+        if level + 1 < len(self.dims) and self.dims[level + 1] in r:
+            self.send(level + 1, "".join(dim for dim in r if dim != self.dims[level + 1]))
+
+    def last(self):
+        level = len(self.dims) - 1
+        self.copy(level, "").wait_recv()
+        return self.received(level, 0)
+
+    def steps(self):
+        return [(level, r) for level in range(len(self.dims) - 1) for r in self.ordered(level)]
+
+    def finish(self):
+        for copy in self.started:
+            copy.wait_send()
+
+
+def dot_nn(left, right):
+    return jnp.dot(left, right, preferred_element_type=F32)
+
+
+def dot_nt(left, right):
+    return lax.dot_general(left, right, (((1,), (1,)), ((), ())), preferred_element_type=F32)
+
+
+def dot_tn(left, right):
+    return lax.dot_general(left, right, (((0,), (0,)), ((), ())), preferred_element_type=F32)
+
+
+def turn(values, cosines, sines):
+    return values * cosines + pltpu.roll(values, values.shape[-1] // 2, 1) * sines
+
+
+def row_scale(values):
+    return lax.rsqrt(jnp.mean(values * values, axis=-1, keepdims=True) + EPS)
+
+def forward_kernel(
+    tokens, cot, w_query, w_key, w_value, w_out, w_gate, w_up, pack, cosines, sines,
+    nf_out, dm_out, gate_out, up_out, packs_out, middle_out, ht_out, wd_out,
+    q_out, k_out, v_out, ql_out, kl_out, att_out, den_out,
+    ht, normed, weights, partial, got_k, got_y, got_z, got_zz, packs, gain,
+    ex_send, ex_recv, w_send, w_recv, fw_send, fw_recv, p_send, p_recv, e_send, e_recv,
+    hs, hr, ds, dr, ss, sr, local,
+):
+    here = my_place()
+    x, tp, ctx = here.x, here.tp, here.ctx
+    mine = w_gate.shape[0] // 8
+    head = cosines.shape[1]
+    started, locals_ = [], []
+
+    def local_copy(source, target):
+        copy = pltpu.make_async_copy(source, target, local.at[len(locals_)])
+        copy.start()
+        locals_.append(copy)
+        return copy
+
+    greet(here)
+    quarter = pl.ds(pl.multiple_of(tp * 16, 16), 16)
+    block_rows = pl.ds(pl.multiple_of(x * 16, 16), 16)
+    other = here.flip("x")
+
+    exchange_copies = []
+    for i, (source, target) in enumerate(((tokens, ht.at[:, here.owner16]), (cot, None))):
+        if target is None:
+            mine_slot, slot_there = dm_out.at[here.z, :, here.owner8], dm_out.at[other.z, :, other.owner8]
+        else:
+            mine_slot, slot_there = target, ht.at[:, other.owner16]
+        copy = remote(
+            source.at[pl.ds(2 * other.x, 2), quarter, :], slot_there.at[:, block_rows, :], ex_send.at[i], ex_recv.at[i], other
+        )
+        copy.start()
+        exchange_copies.append(copy)
+        local_copy(source.at[pl.ds(2 * x, 2), quarter, :], mine_slot.at[:, block_rows, :])
+
+    local_copy(pack, packs.at[ctx])
+    pack_copies = []
+    for step in range(1, 8):
+        copy = remote(pack, packs.at[ctx], p_send.at[step], p_recv.at[step], ctx_peer(here, step))
+        copy.start()
+        pack_copies.append(copy)
+
+    dense = (w_query, w_key, w_value, w_out)
+    my_rows = pl.ds(pl.multiple_of(ctx * 256, 256), 256)
+    w_copies = {}
+
+    def send_weights(which):
+        for j, dims in enumerate(("Z", "z", "Zz")):
+            peer = here.flip(dims)
+            for i in which:
+                copy = remote(
+                    dense[i].at[:, pl.ds(pl.multiple_of(peer.z * head, head), head)],
+                    weights.at[my_rows, pl.ds(i * head, head)],
+                    w_send.at[j, i],
+                    w_recv.at[j, i],
+                    peer,
+                )
+                copy.start()
+                w_copies[j, i] = copy
+
+    own_weights = [
+        local_copy(
+            weight.at[:, pl.ds(pl.multiple_of(here.z * head, head), head)], weights.at[my_rows, pl.ds(i * head, head)]
+        )
+        for i, weight in enumerate(dense)
+    ]
+    forwards = []
+
+    def pass_weights(j, which):
+        place = here.flip(("", "Z", "z", "Zz")[j])
+        if j:
+            for i in which:
+                w_copies[j - 1, i].wait()
+        rows = pl.ds(pl.multiple_of(place.ctx * 256, 256), 256)
+        columns = pl.ds(which[0] * head, len(which) * head)
+        n = 2 * j + (which[0] == 3)
+        copy = remote(weights.at[rows, columns], weights.at[rows, columns], fw_send.at[n], fw_recv.at[n], other)
+        copy.start()
+        forwards.append(copy)
+
+    expert_copies = []
+
+    def send_experts(steps):
+        for i, (weight, target) in enumerate(((w_gate, gate_out), (w_up, up_out))):
+            for step in steps:
+                peer = ctx_peer(here, step)
+                copy = remote(
+                    weight.at[pl.ds(mine * peer.ctx, mine)],
+                    target.at[:, my_rows, :],
+                    e_send.at[i, step],
+                    e_recv.at[i, step],
+                    peer,
+                )
+                copy.start()
+                expert_copies.append(copy)
+
+    for weight, target in ((w_gate, gate_out), (w_up, up_out)):
+        local_copy(weight.at[pl.ds(mine * ctx, mine)], target.at[:, my_rows, :])
+
+    heads = [Gather(here, "Zzyk", lambda place, s=s: ht.at[s, place.owner16], hs.at[s], hr.at[s]) for s in range(2)]
+    marks = [
+        Gather(here, dims, lambda place, s=s: dm_out.at[place.z, s, place.owner8], ds.at[s], dr.at[s])
+        for s, dims in ((0, "Zzxyk"), (1, "Zzyxk"))
+    ]
+    send_weights((0, 1, 2))
+    exchange_copies[0].wait()
+    locals_[0].wait()
+    for gather in heads:
+        gather.send("")
+    exchange_copies[1].wait()
+    locals_[1].wait()
+    for gather in marks:
+        gather.send("")
+    send_weights((3,))
+    for copy in own_weights:
+        copy.wait()
+    pass_weights(0, (0, 1, 2))
+
+    def heads_arrive(*chosen):
+        for r in chosen:
+            for gather in heads:
+                gather.arrive(r)
+
+    def marks_arrive(*chosen):
+        for r in chosen:
+            for gather in marks:
+                gather.arrive(gather.sort(r))
+
+    heads_arrive("Z", "z")
+    pass_weights(1, (0, 1, 2))
+    pass_weights(2, (0, 1, 2))
+    heads_arrive("Zz")
+    pass_weights(3, (0, 1, 2))
+    marks_arrive("Z", "z", "Zz")
+    for j in range(4):
+        pass_weights(j, (3,))
+    send_experts((2, 4, 6))
+    for copy in pack_copies:
+        copy.wait()
+    locals_[2].wait()
+    for i in range(8):
+        gain[0:1, i * 256 : (i + 1) * 256] = packs[i, 16:17, :].astype(F32)
+        gain[1:2, i * 256 : (i + 1) * 256] = packs[i, 17:18, :].astype(F32)
+    qk_gain = jnp.sum(packs[:, 18:20, :head].astype(F32), axis=0)
+    packs_out[...] = packs[...]
+
+    def normalise(i, carry):
+        rows = ht[i // 16, i % 16].astype(F32)
+        target = pl.ds(pl.multiple_of(i * 32, 32), 32)
+        normed[target, :] = (rows * row_scale(rows) * gain[0:1, :]).astype(BF16)
+        return carry
+
+    heads_arrive("y", "Zy", "zy", "Zzy")
+    heads_arrive("k", "Zk", "zk", "Zzk", "yk", "Zyk", "zyk", "Zzyk")
+    lax.fori_loop(0, 32, normalise, 0)
+    for copy in forwards[:4]:
+        copy.wait()
+    save_ht = local_copy(ht, ht_out)
+
+    def project(i, carry):
+        rows = pl.ds(pl.multiple_of(i * 256, 256), 256)
+        table = pl.ds(pl.multiple_of((i % 2) * 256, 256), 256)
+        lin = dot_nn(normed[rows, :], weights[:, : 3 * head])
+        query_lin, key_lin = lin[:, :head], lin[:, head : 2 * head]
+        ql_out[rows, :] = query_lin
+        kl_out[rows, :] = key_lin
+        v_out[rows, :] = lin[:, 2 * head :].astype(BF16)
+        cos, sin = cosines[table, :], sines[table, :]
+        q_out[rows, :] = (
+            turn(query_lin * row_scale(query_lin) * qk_gain[0:1, :], cos, sin) * head ** (-0.5)
+        ).astype(BF16)
+        k_out[rows, :] = turn(key_lin * row_scale(key_lin) * qk_gain[1:2, :], cos, sin).astype(BF16)
+        return carry
+
+    lax.fori_loop(0, 4, project, 0)
+    for copy in forwards[4:]:
+        copy.wait()
+    send_experts((1, 3, 5, 7))
+    save_w = local_copy(weights, wd_out)
+
+    sums = [
+        Scatter(
+            here,
+            "kyzZ",
+            lambda place, s=s: partial.at[s, place.owner16],
+            lambda r, s=s: partial.at[s, here.flip(r).owner16],
+            lambda level, i, s=s: (got_k, got_y, got_z, got_zz)[level].at[s, i],
+            ss.at[s],
+            sr.at[s],
+        )
+        for s in range(2)
+    ]
+    for s in range(2):
+        keys = pl.ds(s * 512, 512)
+
+        def attend(i, carry):
+            rows = pl.ds(pl.multiple_of(s * 512 + i * 256, 256), 256)
+            scores = dot_nt(q_out[rows, :], k_out[keys, :])
+            exponent = jnp.exp(scores)
+            denominator = jnp.sum(exponent, axis=-1, keepdims=True)
+            attended = dot_nn(exponent.astype(BF16), v_out[keys, :]) / denominator
+            att_out[rows, :] = attended.astype(BF16)
+            den_out[rows, :] = jnp.broadcast_to(denominator, attended.shape)
+            attended_low = attended.astype(BF16)
+
+            def column(j, inner):
+                columns = pl.ds(pl.multiple_of(j * 512, 512), 512)
+                term = dot_nt(attended_low, weights[columns, 3 * head :])
+                partial[s, pl.ds(i * 8, 8), :, columns] = term.astype(BF16).reshape(8, 32, 512)
+                return inner
+
+            return lax.fori_loop(0, 4, column, carry)
+
+        lax.fori_loop(0, 2, attend, 0)
+        sums[s].start()
+    def sums_take(level):
+        for one in sums:
+            for r in one.ordered(level):
+                one.take(level, r)
+
+    for r in ("", "Z", "z", "Zz"):
+        marks[0].arrive(r + "x")
+        marks[1].arrive(r + "y")
+    sums_take(0)
+    sums_take(1)
+    for r in ("", "Z", "z", "Zz"):
+        marks[0].arrive(r + "y")
+        marks[1].arrive(r + "x")
+        marks_arrive(r + "xy")
+    sums_take(2)
+    for s in range(2):
+        rest = sums[s].last()
+        total = partial[s, here.owner16].astype(F32) + rest[...].astype(F32)
+        middle = ht[s, here.owner16].astype(F32) + total
+        middle_out[s] = middle
+        nf_out[s] = (middle * row_scale(middle) * gain[1:2, :]).astype(BF16)
+    for r in ("k", "xk", "yk", "xyk"):
+        marks_arrive(r, "Z" + r, "z" + r, "Zz" + r)
+    for copy in expert_copies:
+        copy.wait()
+    for copy in locals_[7:]:
+        copy.wait()
+    for part in heads + marks + sums:
+        part.finish()
+
+
+def forward(tokens, cot, w_query, w_key, w_value, w_out, w_gate, w_up, pack, cosines, sines):
+    anywhere = pl.BlockSpec(memory_space=pl.ANY)
+    vmem = pl.BlockSpec(memory_space=pltpu.VMEM)
+    width = tokens.shape[2]
+    head = cosines.shape[1]
+    mine = w_gate.shape[0] // 8
+    hidden = w_gate.shape[2]
+    all_rows = jax.ShapeDtypeStruct((4, 2, 8, 32, width), BF16)
+    weight = jax.ShapeDtypeStruct((mine, width, hidden), BF16)
+    low, high = jax.ShapeDtypeStruct((1024, head), BF16), jax.ShapeDtypeStruct((1024, head), F32)
+    dma = pltpu.SemaphoreType.DMA
+    return pl.pallas_call(
+        forward_kernel,
+        out_shape=(
+            jax.ShapeDtypeStruct((2, 32, width), BF16), all_rows, weight, weight,
+            jax.ShapeDtypeStruct((8,) + pack.shape, BF16),
+            jax.ShapeDtypeStruct((2, 32, width), F32),
+            jax.ShapeDtypeStruct((2, 16, 32, width), BF16),
+            jax.ShapeDtypeStruct((width, 4 * head), BF16),
+            low, low, low, high, high, low, high,
+        ),
+        in_specs=[anywhere] * 9 + [vmem] * 2,
+        out_specs=(vmem,) + (anywhere,) * 3 + (vmem, vmem) + (anywhere,) * 2 + (vmem,) * 7,
+        scratch_shapes=[
+            pltpu.VMEM((2, 16, 32, width), BF16),
+            pltpu.VMEM((1024, width), BF16),
+            pltpu.VMEM((width, 4 * head), BF16),
+            pltpu.VMEM((2, 16, 32, width), BF16),
+            pltpu.VMEM((2, 8, 32, width), BF16),
+            pltpu.VMEM((2, 4, 32, width), BF16),
+            pltpu.VMEM((2, 2, 32, width), BF16),
+            pltpu.VMEM((2, 1, 32, width), BF16),
+            pltpu.VMEM((8,) + pack.shape, BF16),
+            pltpu.VMEM((8, width), F32),
+            dma((2,)), dma((2,)), dma((3, 4)), dma((3, 4)), dma((8,)), dma((8,)), dma((8,)), dma((8,)),
+            dma((3, 8)), dma((3, 8)), dma((2, 16)), dma((2, 16)), dma((2, 32)), dma((2, 32)),
+            dma((2, 16)), dma((2, 16)), dma((16,)),
+        ],
+        compiler_params=pltpu.CompilerParams(collective_id=0, has_side_effects=True, vmem_limit_bytes=VMEM_LIMIT),
+        cost_estimate=pl.CostEstimate(flops=4 * 10**9, bytes_accessed=64 * 10**6, transcendentals=10**6),
+    )(tokens, cot, w_query, w_key, w_value, w_out, w_gate, w_up, pack, cosines, sines)
+
+def norm_gradient(gradient, values, scale, gain):
+    weighted = gradient * gain
+    return scale * weighted - values * (scale * scale * scale * jnp.mean(weighted * values, axis=-1, keepdims=True))
+
+
+Z_PARTS = ("", "Zz", "z", "Z")
+Z_ORDER = ("Zz", "z", "Z", "")
+
+
+def later_kernel(
+    nf_own, dm_in, gate_in, up_in, down_in, packs, chosen, middle, ht_in, wd_in,
+    q_in, k_in, v_in, ql_in, kl_in, att_in, den_in, cosines, sines,
+    layer_out, input_grad, gate_out, up_out, down_out, dense_out, mixed_out, small_out,
+    nf, dm, part, w_gate, w_up, w_down, grad_down, hidden, active, grad_gate, grad_up, grad_logits, router, stage,
+    got_k, got_a, got_b, got_z, got_zz, gain, grad_middle, lin_t, key_sum, value_sum, scales, columns_sum, qk_sum, sg, sg_k, sg_y, sg_all,
+    ns, nr, rs, rr, e_send, e_recv, hs, hr, ms, mr, ss, sr, o_send, o_recv, o2_send, o2_recv, d_send, d_recv, g_send, g_recv,
+    local, stage_sem, ready,
+):
+    here = my_place()
+    x, tp, ctx = here.x, here.tp, here.ctx
+    other = here.flip("x")
+    width = nf.shape[4]
+    head = cosines.shape[1]
+    experts = packs.shape[1] - 32
+    mine = w_gate.shape[0]
+    locals_ = []
+
+    def local_copy(source, target):
+        copy = pltpu.make_async_copy(source, target, local.at[len(locals_)])
+        copy.start()
+        locals_.append(copy)
+        return copy
+
+    own_copy = local_copy(nf_own, nf.at[here.z, :, here.owner8])
+    loads = [local_copy(gate_in, w_gate), local_copy(up_in, w_up), local_copy(chosen, grad_logits)]
+    dm_load = local_copy(dm_in, dm)
+    greet(here)
+    gathers = [
+        Gather(here, dims, lambda place, s=s: nf.at[place.z, s, place.owner8], ns.at[s], nr.at[s], nf_own.at[s])
+        for s, dims in ((0, "Zzxyk"), (1, "Zzyxk"))
+    ]
+    for gather in gathers:
+        gather.send("")
+    quarter = pl.ds(pl.multiple_of(tp * 16, 16), 16)
+    block_rows = pl.ds(pl.multiple_of(x * 16, 16), 16)
+    other_rows = pl.ds(pl.multiple_of(other.x * 16, 16), 16)
+    my_rows = pl.ds(pl.multiple_of(ctx * 256, 256), 256)
+    down_copies = [local_copy(down_in.at[pl.ds(mine * ctx, mine)], w_down.at[:, my_rows, :])]
+
+    def send_down(steps):
+        for step in steps:
+            peer = ctx_peer(here, step)
+            copy = remote(
+                down_in.at[pl.ds(mine * peer.ctx, mine)], w_down.at[:, my_rows, :], e_send.at[0, step], e_recv.at[0, step], peer
+            )
+            copy.start()
+            down_copies.append(copy)
+
+    router[...] = jnp.zeros_like(router)
+    for i in range(8):
+        columns = slice(i * 256, (i + 1) * 256)
+        router[0:experts, columns] = packs[i, 0:experts, :]
+        gain[0:1, columns] = packs[i, 16:17, :].astype(F32)
+        gain[1:2, columns] = packs[i, 17:18, :].astype(F32)
+    qk_gain = jnp.sum(packs[:, 18:20, :head].astype(F32), axis=0)
+
+    def arrive(s, *chosen_ones):
+        for r in chosen_ones:
+            gathers[s].arrive(gathers[s].sort(r))
+
+    parts = [
+        Scatter(
+            here,
+            dims,
+            lambda place, s=s: part.at[place.z, s, place.owner8],
+            lambda r, s=s: part.at[here.flip(r).z, s, here.flip(r).owner8],
+            lambda level, i, s=s: (got_k, got_a, got_b, got_z, got_zz)[level].at[s, i],
+            rs.at[s],
+            rr.at[s],
+        )
+        for s, dims in enumerate(ALL_ORDERS)
+    ]
+
+    def in_part(s, level, z_part):
+        inner = parts[s].dims[level + 1 : 3]
+        return [r for r in parts[s].ordered(level) if set(r) == (set(r) & set(inner)) | set(z_part)]
+
+    def take(level, z_part):
+        for s in range(2):
+            for r in in_part(s, level, z_part):
+                parts[s].take(level, r)
+
+    lanes = lax.broadcasted_iota(jnp.int32, (256, 128), 1)
+
+    def weights_of(rows):
+        logits = jnp.where(lanes < experts, dot_nt(rows, router[...]), -1e30)
+        expo = jnp.exp(logits - jnp.max(logits, axis=-1, keepdims=True))
+        return expo / jnp.sum(expo, axis=-1, keepdims=True)
+
+    def first_pass(z, s):
+        flat = pl.ds(pl.multiple_of(z * 512 + s * 256, 256), 256)
+        rows = nf[z, s].reshape(256, width)
+        probs = weights_of(rows)
+        picked = probs * grad_logits[flat, :].astype(F32)
+        for e in range(mine):
+            gate = jnp.sum(picked * (lanes == here.ctx * mine + e).astype(F32), axis=-1, keepdims=True)
+            gate_pre, up_pre = dot_nn(rows, w_gate[e]), dot_nn(rows, w_up[e])
+            sigmoid_gate = jax.nn.sigmoid(gate_pre)
+            silu_gate = gate_pre * sigmoid_gate
+            activated = silu_gate * up_pre
+            hidden[e, flat, :] = (gate * activated).astype(BF16)
+            active[e, flat, :] = activated.astype(BF16)
+            grad_up[e, flat, :] = silu_gate.astype(BF16)
+            grad_gate[e, flat, :] = (up_pre * sigmoid_gate * (1.0 + gate_pre * (1.0 - sigmoid_gate))).astype(BF16)
+
+    def second_pass(z, s):
+        flat = pl.ds(pl.multiple_of(z * 512 + s * 256, 256), 256)
+        grad_rows = dm[z, s].reshape(256, width)
+        probs = weights_of(nf[z, s].reshape(256, width))
+        picked = grad_logits[flat, :].astype(F32)
+        placed = jnp.zeros((256, 128), F32)
+        for e in range(mine):
+            this = (lanes == here.ctx * mine + e).astype(F32)
+            named = jnp.sum(picked * this, axis=-1, keepdims=True)
+            gate = jnp.sum(probs * this, axis=-1, keepdims=True) * named
+            grad_hidden = dot_nn(grad_rows, w_down[e])
+            dot = jnp.sum(grad_hidden * active[e, flat, :].astype(F32), axis=-1, keepdims=True)
+            placed = placed + dot * named * this
+            grad_act = gate * grad_hidden
+            grad_up[e, flat, :] = (grad_act * grad_up[e, flat, :].astype(F32)).astype(BF16)
+            grad_gate[e, flat, :] = (grad_act * grad_gate[e, flat, :].astype(F32)).astype(BF16)
+        share = (probs * (placed - jnp.sum(probs * placed, axis=-1, keepdims=True))).astype(BF16)
+        grad_logits[flat, :] = share
+
+        def column(j, carry):
+            columns = pl.ds(pl.multiple_of(j * 512, 512), 512)
+            term = dot_nn(share, router[:, columns])
+            mixed = jnp.zeros((256, 512), F32)
+            for e in range(mine):
+                mixed = mixed + dot_nt(hidden[e, flat, :], w_down[e, columns, :])
+                term = term + dot_nt(grad_gate[e, flat, :], w_gate[e, columns, :])
+                term = term + dot_nt(grad_up[e, flat, :], w_up[e, columns, :])
+            stage[s, :, :, columns] = mixed.astype(BF16).reshape(8, 32, 512)
+            part[z, s, :, :, columns] = term.astype(BF16).reshape(8, 32, 512)
+            return carry
+
+        lax.fori_loop(0, width // 512, column, 0)
+
+    for number, z_part in enumerate(Z_PARTS):
+        if number == 0:
+            arrive(0, "x")
+            arrive(1, "y")
+            for s in range(2):
+                arrive(s, "Z", "z")
+            arrive(0, "y", "xy")
+            arrive(1, "x", "xy")
+            for s in range(2):
+                arrive(s, "Zz")
+            send_down((2, 4, 6))
+            for r in ("k", "xk", "yk", "xyk"):
+                for s in range(2):
+                    arrive(s, r)
+            own_copy.wait()
+            for copy in loads:
+                copy.wait()
+        else:
+            if number == 1:
+                for z_other in Z_PARTS[1:]:
+                    arrive(0, z_other + "x")
+                    arrive(1, z_other + "y")
+                send_down((1, 3, 5, 7))
+            for inner in ("x", "y", "xy", "k", "xk", "yk", "xyk"):
+                for s in range(2):
+                    if inner != ("x", "y")[s]:
+                        arrive(s, z_part + inner)
+        z = here.flip(z_part).z
+
+        def both(s, carry):
+            first_pass(z, s)
+            return carry
+
+        lax.fori_loop(0, 2, both, 0)
+    dm_load.wait()
+    def weigh_down(i, carry):
+        columns = pl.ds(pl.multiple_of(i * 256, 256), 256)
+        grad_rows = dm[:, :, :, :, columns].reshape(2048, 256)
+        for e in range(mine):
+            grad_down[e, columns, :] = dot_tn(grad_rows, hidden[e]).astype(BF16)
+        return carry
+
+    lax.fori_loop(0, 8, weigh_down, 0)
+    for copy in down_copies:
+        copy.wait()
+    give_copies = [local_copy(grad_down.at[:, my_rows, :], down_out.at[pl.ds(mine * ctx, mine)])]
+    queue = [(1, grad_down, down_out, step) for step in (2, 4, 6, 1, 3, 5, 7)]
+    for step in (2, 4, 6, 1, 3, 5, 7):
+        queue += [(2, w_gate, gate_out, step), (3, w_up, up_out, step)]
+
+    def give(count):
+        for which, source, target, step in queue[:count]:
+            peer = ctx_peer(here, step)
+            rows = pl.ds(pl.multiple_of(peer.ctx * 256, 256), 256)
+            copy = remote(
+                source.at[:, rows, :], target.at[pl.ds(mine * ctx, mine)], e_send.at[which, step], e_recv.at[which, step], peer
+            )
+            copy.start()
+            give_copies.append(copy)
+        del queue[:count]
+
+    give(3)
+    stage_copy = None
+    for number, z_part in enumerate(Z_ORDER):
+        z = here.flip(z_part).z
+        if stage_copy is not None:
+            stage_copy.wait()
+
+        def both_again(s, carry):
+            second_pass(z, s)
+            return carry
+
+        lax.fori_loop(0, 2, both_again, 0)
+        stage_copy = pltpu.make_async_copy(stage, mixed_out.at[z], stage_sem.at[0])
+        stage_copy.start()
+        for s in range(2):
+            for r in in_part(s, 0, z_part):
+                parts[s].send(0, r)
+        if number >= 1:
+            take(0, Z_ORDER[number - 1])
+        if number >= 2:
+            take(1, Z_ORDER[number - 2])
+        if number >= 3:
+            take(2, Z_ORDER[number - 3])
+        if number >= 1:
+            give(1)
+
+    def weigh(step):
+        i = (ctx + step) % 8
+        columns = pl.ds(pl.multiple_of(i * 256, 256), 256)
+        rows = nf[:, :, :, :, columns].reshape(2048, 256)
+        for e in range(mine):
+            w_gate[e, columns, :] = dot_tn(rows, grad_gate[e]).astype(BF16)
+            w_up[e, columns, :] = dot_tn(rows, grad_up[e]).astype(BF16)
+        sg[i, 0:16, :] = dot_tn(grad_logits[...], rows)[0:16, :]
+
+    def weigh_some(start, stop, stride, offset):
+        def one(n, carry):
+            weigh(n * stride + offset)
+            return carry
+
+        lax.fori_loop(start, stop, one, 0)
+
+    weigh_some(1, 2, 2, 0)
+    take(0, Z_ORDER[3])
+    take(1, Z_ORDER[2])
+    take(2, Z_ORDER[1])
+    weigh_some(2, 4, 2, 0)
+    take(1, Z_ORDER[3])
+    take(2, Z_ORDER[2])
+    for s in range(2):
+        parts[s].take(3, "Z")
+    weigh_some(0, 3, 2, 1)
+    take(2, Z_ORDER[3])
+    for s in range(2):
+        parts[s].take(3, "")
+    weigh_some(3, 4, 2, 1)
+    weigh_some(0, 1, 2, 0)
+    give(1)
+    stage_copy.wait()
+    for one in gathers:
+        one.finish()
+    for s in range(2):
+        stage[s, 0] = dm[here.z, s, here.owner8]
+    load_w = [local_copy(wd_in.at[:, pl.ds(n * 256, 256)], w_down.at[n]) for n in range(2)]
+    load_ht = local_copy(ht_in, nf.at[pl.ds(0, 2)])
+    load_w += [local_copy(q_in, grad_logits.at[pl.ds(0, 1024)]), local_copy(k_in, grad_logits.at[pl.ds(1024, 1024)])]
+    for peer in everyone(here):
+        pl.semaphore_signal(ready, inc=1, device_id=peer.device, device_id_type=MESH_ID)
+
+    own8, own_half = here.owner16 % 8, here.owner16 // 8
+    mixed, loads = [], []
+    for s, dims in enumerate(ALL_ORDERS):
+
+        def index(r, dims=dims):
+            return sum(1 << dims[1:].index(dim) for dim in r)
+
+        def landing(level, i, s=s):
+            if level == 0:
+                return nf.at[2 + s, i // 8, i % 8]
+            return got_k.at[s, (0, 0, 8, 12, 14)[level] + i]
+
+        mixed.append(
+            Scatter(
+                here,
+                dims,
+                lambda place, s=s: mixed_out.at[place.z, s, place.owner8],
+                lambda r, s=s, index=index: dm.at[2 + s, index(r) // 8, index(r) % 8],
+                landing,
+                ms.at[s],
+                mr.at[s],
+            )
+        )
+        for r in mixed[s].ordered(0):
+            there = here.flip(r)
+            loads.append(local_copy(mixed_out.at[there.z, s, there.owner8], mixed[s].slot(r)))
+
+    def mixed_take(level, which=(0, 1)):
+        for s in which:
+            for r in mixed[s].ordered(level):
+                mixed[s].take(level, r)
+
+    columns_sum[...] = jnp.zeros_like(columns_sum)
+    for s in range(2):
+        gradient = part[here.z, s, here.owner8].astype(F32) + parts[s].last()[...].astype(F32)
+        values = middle[s]
+        scale = row_scale(values)
+        columns_sum[1:2, :] += jnp.sum(gradient * values * scale, axis=0, keepdims=True)
+        total = stage[s, 0].astype(F32) + norm_gradient(gradient, values, scale, gain[1:2, :])
+        grad_middle[s] = total
+        stage[s, 1] = total.astype(BF16)
+    heads = [
+        Gather(
+            here, "Zzyk", lambda place, s=s: dm.at[s, place.owner16 // 8, place.owner16 % 8], hs.at[s], hr.at[s], stage.at[s, 1]
+        )
+        for s in range(2)
+    ]
+    for one in parts:
+        one.finish()
+    pl.semaphore_wait(ready, len(everyone(here)))
+    for gather in heads:
+        gather.send("")
+    own_copy = local_copy(stage.at[:, 1], dm.at[pl.ds(0, 2), own_half, own8])
+    for one in mixed:
+        one.start()
+    give_copies.append(local_copy(w_gate.at[:, my_rows, :], gate_out.at[pl.ds(mine * ctx, mine)]))
+    give_copies.append(local_copy(w_up.at[:, my_rows, :], up_out.at[pl.ds(mine * ctx, mine)]))
+    for r in ("Z", "z", "Zz"):
+        for gather in heads:
+            gather.arrive(r)
+    give(3)
+    load_ht.wait()
+
+    def normalise(i, carry):
+        s, a, c = i // 16, (i % 16) // 8, i % 8
+        rows = nf[s, a, c].astype(F32)
+        scale = row_scale(rows)
+        scales[pl.ds(pl.multiple_of(i * 32, 32), 32), :] = jnp.broadcast_to(scale, (32, head))
+        part[2 + s, a, c] = (rows * scale * gain[0:1, :]).astype(BF16)
+        return carry
+
+    lax.fori_loop(0, 32, normalise, 0)
+    give(1)
+    for copy in loads:
+        copy.wait()
+    mixed_take(0, (1,))
+    for r in heads[0].order():
+        if r not in ("Z", "z", "Zz"):
+            for gather in heads:
+                gather.arrive(r)
+    own_copy.wait()
+    for copy in load_w:
+        copy.wait()
+
+    give(2)
+    qk_sum[...] = jnp.zeros_like(qk_sum)
+    score_scale = head ** (-0.5)
+    for s in range(2):
+        all_rows = pl.ds(s * 512, 512)
+        upper_rows = pl.ds(1024 + s * 512, 512)
+        key_sum[...] = jnp.zeros_like(key_sum)
+        value_sum[...] = jnp.zeros_like(value_sum)
+
+        def attend(i, carry):
+            rows = pl.ds(pl.multiple_of(s * 512 + i * 256, 256), 256)
+            upper = pl.ds(pl.multiple_of(1024 + s * 512 + i * 256, 256), 256)
+            table = pl.ds(pl.multiple_of(i * 256, 256), 256)
+            gradient = dot_nn(dm[s, i].reshape(256, width), w_down[1, :, head:])
+            attended, denominator = att_in[rows, :].astype(F32), den_in[rows, :]
+            active[0, upper, head:] = att_in[rows, :]
+            exponent = jnp.exp(dot_nt(grad_logits[rows, :], grad_logits[upper_rows, :]))
+            grad_acc = (gradient / denominator).astype(BF16)
+            grad_total = -jnp.sum(gradient * attended, axis=-1, keepdims=True) / denominator[:, :1]
+            grad_prob = dot_nt(grad_acc, v_in[all_rows, :])
+            grad_score = (exponent * (grad_prob + grad_total)).astype(BF16)
+            grad_query = dot_nn(grad_score, grad_logits[upper_rows, :]) * score_scale
+            key_sum[...] += dot_tn(grad_score, grad_logits[rows, :])
+            value_sum[...] += dot_tn(exponent.astype(BF16), grad_acc)
+            grad_query = turn(grad_query, cosines[table, :], -sines[table, :])
+            values = ql_in[rows, :]
+            scale = row_scale(values)
+            qk_sum[0:1, :] += jnp.sum(grad_query * values * scale, axis=0, keepdims=True)
+            active[0, rows, :head] = norm_gradient(grad_query, values, scale, qk_gain[0:1, :]).astype(BF16)
+            return carry
+
+        lax.fori_loop(0, 2, attend, 0)
+        grad_keys = turn(key_sum[...], cosines[...], -sines[...])
+        values = kl_in[all_rows, :]
+        scale = row_scale(values)
+        qk_sum[1:2, :] += jnp.sum(grad_keys * values * scale, axis=0, keepdims=True)
+        active[0, all_rows, head:] = norm_gradient(grad_keys, values, scale, qk_gain[1:2, :]).astype(BF16)
+        active[0, upper_rows, :head] = value_sum[...].astype(BF16)
+
+    give(1)
+    sums = [
+        Scatter(
+            here,
+            "kyzZ",
+            lambda place, s=s: part.at[s, place.owner16 // 8, place.owner16 % 8],
+            lambda r, s=s: part.at[s, here.flip(r).owner16 // 8, here.flip(r).owner16 % 8],
+            lambda level, i, s=s: (got_a, got_b, got_z, got_zz)[level].at[s, i],
+            ss.at[s],
+            sr.at[s],
+        )
+        for s in range(2)
+    ]
+    for s in range(2):
+
+        def project(n, carry):
+            i, j = n // 4, n % 4
+            rows = pl.ds(pl.multiple_of(s * 512 + i * 256, 256), 256)
+            upper = pl.ds(pl.multiple_of(1024 + s * 512 + i * 256, 256), 256)
+            columns = pl.ds(pl.multiple_of(j * 512, 512), 512)
+            term = dot_nt(active[0, rows, :], w_down[0, columns, :])
+            term = term + dot_nt(active[0, upper, :head], w_down[1, columns, :head])
+            unit = nf[s, i, :, :, columns].reshape(256, 512).astype(F32) * scales[rows, :1]
+            columns_sum[0:1, columns] += jnp.sum(term * unit, axis=0, keepdims=True)
+            part[s, i, :, :, columns] = term.astype(BF16).reshape(8, 32, 512)
+            return carry
+
+        lax.fori_loop(0, 8, project, 0)
+        sums[s].start()
+
+    give(1)
+    for one in sums:
+        for r in one.ordered(0):
+            one.take(0, r)
+
+    def slot(i):
+        return hidden.at[i // 4, pl.ds(pl.multiple_of((i % 4) * 512, 512), 512), :]
+
+    for i in range(4):
+        rows, upper = slice(i * 256, (i + 1) * 256), slice(1024 + i * 256, 1280 + i * 256)
+        lin_t[0 : 2 * head, rows] = active[0, rows, :].T
+        lin_t[2 * head :, rows] = active[0, upper, :].T
+
+    def weigh_dense(i, carry):
+        columns = pl.ds(pl.multiple_of(i * 256, 256), 256)
+        start = (i % 4) * 512
+        rows = part[2:4, :, :, :, columns].reshape(1024, 256)
+        term = dot_nn(lin_t[: 3 * head, :], rows).astype(BF16)
+        hidden[i // 4, pl.ds(pl.multiple_of(start, 128), 3 * head), :] = term
+        return carry
+
+    def weigh_out(i, carry):
+        columns = pl.ds(pl.multiple_of(i * 256, 256), 256)
+        start = (i % 4) * 512 + 3 * head
+        rows = dm[0:2, :, :, :, columns].reshape(1024, 256)
+        term = dot_nn(lin_t[3 * head :, :], rows).astype(BF16)
+        hidden[i // 4, pl.ds(pl.multiple_of(start, 128), head), :] = term
+        return carry
+
+    lax.fori_loop(0, 8, weigh_dense, 0)
+    lax.fori_loop(0, 8, weigh_out, 0)
+
+    def across(n):
+        return grad_gate.at[0, pl.ds(n * 512, 512), :]
+
+    def along(n):
+        return grad_gate.at[1, pl.ds(n * 512, 512), :]
+
+    dense_copies = []
+    for i, dims in enumerate(("", "Z", "z", "Zz")):
+        copy = remote(slot(other.flip(dims).ctx), across(i), d_send.at[i], d_recv.at[i], other)
+        copy.start()
+        dense_copies.append(copy)
+
+    for i in range(8):
+        columns = slice(i * 256, (i + 1) * 256)
+        sg[i, 16:18, :] = columns_sum[0:2, columns]
+        sg[i, 18:20, :head] = qk_sum[0:2, :]
+        sg[i, 18:20, head:] = jnp.zeros((2, 256 - head), F32)
+        sg[i, 20:24, :] = jnp.zeros((4, 256), F32)
+    sg_copies = [remote(sg, sg_k, g_send.at[0], g_recv.at[0], here.flip("k"))]
+    sg_copies[0].start()
+    give(2)
+    for one in sums:
+        for r in one.ordered(1):
+            one.take(1, r)
+    sg_copies[0].wait()
+    sg[...] = sg[...] + sg_k[...]
+    sg_copies.append(remote(sg, sg_y, g_send.at[8], g_recv.at[8], here.flip("y")))
+    sg_copies[1].start()
+    mixed_take(0, (0,))
+    mixed_take(1, (1,))
+    for one in sums:
+        for r in one.ordered(2):
+            one.take(2, r)
+    for s in range(2):
+        gradient = part[s, own_half, own8].astype(F32) + sums[s].last()[...].astype(F32)
+        values = nf[s, own_half, own8].astype(F32)
+        total = grad_middle[s] + norm_gradient(gradient, values, row_scale(values), gain[0:1, :])
+        stage[s, 3] = total.astype(BF16)
+
+    hands, hand_locals = [], []
+
+    def hand_out(owned, target, sends, receives):
+        cross = remote(
+            owned.at[:, other_rows, :], target.at[pl.ds(2 * x, 2), quarter, :], sends.at[2, 0], receives.at[2, 0], other
+        )
+        cross.start()
+        parts = [
+            Gather(
+                here,
+                "yk",
+                lambda place, which=which: target.at[
+                    pl.ds(2 * which, 2), pl.ds(pl.multiple_of(place.tp * 16, 16), 16), :
+                ],
+                sends.at[i],
+                receives.at[i],
+                own,
+            )
+            for i, (which, own) in enumerate(((x, owned.at[:, block_rows, :]), (other.x, None)))
+        ]
+        parts[0].send("")
+        hand_locals.append(local_copy(owned.at[:, block_rows, :], target.at[pl.ds(2 * x, 2), quarter, :]))
+        hands.append((cross, parts))
+
+    def hand_on(cross, parts):
+        cross.wait()
+        parts[1].send("")
+        for r in parts[0].order():
+            for part in parts:
+                part.arrive(r)
+        for part in parts:
+            part.finish()
+
+    hand_out(stage.at[:, 3], input_grad, o_send, o_recv)
+    give(1)
+    sg_copies[1].wait()
+    sg[...] = sg[...] + sg_y[...]
+    for step in range(1, 8):
+        peer = ctx_peer(here, step)
+        copy = remote(sg.at[peer.ctx], sg_all.at[ctx], g_send.at[step], g_recv.at[step], peer)
+        copy.start()
+        sg_copies.append(copy)
+    for copy in dense_copies:
+        copy.wait()
+    z_copies = []
+    for i, dims in enumerate(("Z", "z", "Zz", "")):
+        place = here.flip(dims)
+        add_blocks(slot(place.ctx), slot(place.ctx), across(("", "Z", "z", "Zz").index(dims)))
+        if dims:
+            copy = remote(slot(place.ctx), along(i), d_send.at[4 + i], d_recv.at[4 + i], place)
+            copy.start()
+            z_copies.append((dims, copy))
+    mixed_take(1, (0,))
+    mixed_take(2)
+    hand_on(*hands[0])
+    mixed_take(3)
+    give(len(queue))
+    for s in range(2):
+        total = dm[2 + s, 0, 0].astype(F32) + mixed[s].last()[...].astype(F32)
+        stage[s, 2] = (middle[s] + total).astype(BF16)
+    hand_out(stage.at[:, 2], layer_out, o2_send, o2_recv)
+    saves = [local_copy(slot(ctx), dense_out.at[here.z])]
+    for i, (dims, copy) in enumerate(z_copies):
+        copy.wait()
+        saves.append(local_copy(along(i), dense_out.at[here.flip(dims).z]))
+    for copy in sg_copies[2:]:
+        copy.wait()
+    sg_all[ctx] = sg[ctx]
+    small_out[...] = jnp.sum(sg_all[...], axis=0)
+    hand_on(*hands[1])
+    for copy in give_copies + hand_locals + saves:
+        copy.wait()
+    for one in heads + mixed + sums:
+        one.finish()
+
+
+def later(*arrays):
+    nf_own, dm, gate_w, up_w, raw_down = arrays[:5]
+    anywhere = pl.BlockSpec(memory_space=pl.ANY)
+    vmem = pl.BlockSpec(memory_space=pltpu.VMEM)
+    width, head = nf_own.shape[2], arrays[10].shape[1]
+    mine, _, units = gate_w.shape
+    dma = pltpu.SemaphoreType.DMA
+    all_rows = (4, 2, 8, 32, width)
+    tokens = jax.ShapeDtypeStruct((4, 64, width), BF16)
+    expert = jax.ShapeDtypeStruct(raw_down.shape, BF16)
+    return pl.pallas_call(
+        later_kernel,
+        out_shape=(
+            tokens, tokens, expert, expert, expert,
+            jax.ShapeDtypeStruct((4, 4 * head, 256), BF16),
+            jax.ShapeDtypeStruct(all_rows, BF16),
+            jax.ShapeDtypeStruct((24, 256), F32),
+        ),
+        in_specs=[anywhere] * 5 + [vmem, anywhere, vmem] + [anywhere] * 4 + [vmem] * 7,
+        out_specs=(anywhere,) * 7 + (vmem,),
+        scratch_shapes=[
+            *[pltpu.VMEM(all_rows, BF16) for _ in range(3)],
+            *[pltpu.VMEM(gate_w.shape, BF16) for _ in range(4)],
+            *[pltpu.VMEM((mine, 2048, units), BF16) for _ in range(4)],
+            pltpu.VMEM((2048, 128), BF16),
+            pltpu.VMEM((128, width), BF16),
+            pltpu.VMEM((2, 8, 32, width), BF16),
+            *[pltpu.VMEM((2, n, 32, width), BF16) for n in (16, 8, 4, 2, 1)],
+            pltpu.VMEM((8, width), F32),
+            pltpu.VMEM((2, 32, width), F32),
+            pltpu.VMEM((4 * head, 1024), BF16),
+            pltpu.VMEM((512, head), F32),
+            pltpu.VMEM((512, head), F32),
+            pltpu.VMEM((1024, head), F32),
+            pltpu.VMEM((8, width), F32),
+            pltpu.VMEM((8, head), F32),
+            *[pltpu.VMEM((8, 24, 256), F32) for _ in range(4)],
+            dma((2, 32)), dma((2, 32)), dma((2, 32)), dma((2, 32)), dma((4, 8)), dma((4, 8)), dma((2, 16)), dma((2, 16)),
+            dma((2, 32)), dma((2, 32)), dma((2, 16)), dma((2, 16)), dma((3, 4)), dma((3, 4)), dma((3, 4)), dma((3, 4)),
+            dma((8,)), dma((8,)), dma((9,)), dma((9,)), dma((64,)), dma((1,)), pltpu.SemaphoreType.REGULAR,
+        ],
+        compiler_params=pltpu.CompilerParams(
+            collective_id=1, has_side_effects=True, vmem_limit_bytes=VMEM_LIMIT
+        ),
+        cost_estimate=pl.CostEstimate(flops=48 * 10**9, bytes_accessed=64 * 10**6, transcendentals=10**6),
+    )(*arrays)
+
+ALL_ORDERS = ("kyxzZ", "kxyzZ")
+
+
+def per_device_fast(
+    tokens, cotangent, routes, attn_gain, ffn_gain, qk_gain, w_query, w_key, w_value, w_out, router, w_gate, w_up, w_down
+):
+    width = tokens.shape[2]
+    head_size = qk_gain.shape[0] * 8
+    half_size = head_size // 2
+    experts = w_gate.shape[0]
+    mine = experts // 8
+    hidden_units = w_gate.shape[2]
+    ctx, tp = lax.axis_index("ctx"), lax.axis_index("tp")
+    z, x = ctx // 2, ctx % 2
+    f32, bf16 = F32, BF16
+
+    chosen = jnp.sum((routes[..., None] == jnp.arange(experts)).astype(bf16), axis=2)
+    spots = (jnp.arange(head_size)[None, :] == (ctx * 16 + jnp.arange(16))[:, None]).astype(bf16)
+    qk_rows = jnp.einsum("gc,gh->ch", qk_gain, spots, preferred_element_type=f32).astype(bf16)
+    columns = jnp.concatenate(
+        [router, attn_gain[:, None], ffn_gain[:, None], jnp.zeros((256, 14), bf16), chosen.reshape(-1, experts)], axis=1
+    )
+    pack = columns.T + jnp.pad(qk_rows, ((18, 28), (0, 256 - head_size)))
+
+    zs, ys, ks, bs, i = np.meshgrid(np.arange(4), np.arange(2), np.arange(2), np.arange(2), np.arange(16), indexing="ij")
+    positions = ((zs * 2 + bs) * 64 + (ys * 2 + ks) * 16 + i).reshape(-1).astype(np.float32)
+    exponents = np.float32(-2.0) * np.arange(half_size).astype(np.float32) / np.float32(head_size)
+    angles = positions[:, None] * (np.float32(ROPE_BASE) ** exponents)[None, :]
+    cosines = jnp.asarray(np.tile(np.cos(angles), (1, 2)))
+    sines = jnp.asarray(np.concatenate([-np.sin(angles), np.sin(angles)], axis=1))
+
+    (
+        nf, dm, gate_w, up_w, packs, middle, head_tokens, dense, query, keys, value_rows, query_lin, key_lin, attended, denominator,
+    ) = forward(tokens, cotangent, w_query, w_key, w_value, w_out, w_gate, w_up, pack, cosines, sines)
+
+    chosen = packs[:, 32:48].reshape(4, 2, experts, 2, 2, 4, 16)
+    chosen = jnp.transpose(chosen, (0, 4, 3, 5, 1, 6, 2)).reshape(-1, experts)
+    chosen = jnp.pad(chosen, ((0, 0), (0, 128 - experts)))
+    layer_out, input_grad, grad_gate_w, grad_up_w, grad_down_w, dense_grad, _, small = later(
+        nf, dm, gate_w, up_w, w_down, packs, chosen, middle, head_tokens.reshape(2, 2, 8, 32, width), dense,
+        query, keys, value_rows, query_lin, key_lin, attended, denominator, cosines, sines,
+    )
+    dense_grad = jnp.transpose(dense_grad.astype(f32).reshape(4, 4, head_size, 256), (1, 3, 0, 2)).reshape(4, 256, 4 * head_size)
+    return (
+        layer_out,
+        input_grad,
+        small[16],
+        small[17],
+        lax.dynamic_slice_in_dim(small[18:20], ctx * 16, 16, 1).T,
+        dense_grad[0],
+        dense_grad[1],
+        dense_grad[2],
+        dense_grad[3],
+        small[:experts].T,
+        grad_gate_w.astype(f32),
+        grad_up_w.astype(f32),
+        grad_down_w.astype(f32),
+    )
+
+
 def solution(mesh):
+    fast = mesh.shape["ctx"] == 8 and mesh.shape["tp"] == 4
     return jax.shard_map(
-        per_device,
+        per_device_fast if fast else per_device,
         mesh=mesh,
         in_specs=(
             P(None, "ctx", None),

time: 2960 us -> 553 us (0.19)
  waiting for transfers between devices: 2250 us -> 0 us
  Pallas kernels: 0 us -> 512 us
  matrix products: 320 us -> 0.19 us
  other arithmetic: 155 us -> 10.2 us
  blocking collectives: 109 us -> 0 us
  local copies, waits for them, and re-layouts: 99.1 us -> 19.4 us
    reduce_scatter x12 -> x0, waiting for transfers between devices: 1250 us -> none  [the longest x1 285 us: reduce_grads(): lax.psum_scatter(expert_grads[0].astype(jnp.bfloat16), 'ctx', scatter_dim...]
    all_gather x11 -> x0, waiting for transfers between devices: 908 us -> none  [the longest x1 218 us: fetch_experts(): lax.all_gather(w_gate, 'ctx', axis=1, tiled=True)]
    pallas_call x0 -> x2, Pallas kernels: none -> 512 us  [the longest x1 347 us: later(): pl.pallas_call(later_kernel, out_shape=(tokens, tokens, expert, expert, e...]
    dot_general x60 -> x1, matrix products: 320 us -> 0.19 us  [per_device_fast(): jnp.einsum('gc,gh->ch', qk_gain, spots, preferred_element_type=f32)]
    scatter-add x4 -> x0, other arithmetic: 87.2 us -> none  [the longest x2 43.9 us: per_device(): grad_normed_part = jnp.zeros((row_count, model_width), jnp.float32).at[so...]
    psum x3 -> x0, waiting for transfers between devices: 81.2 us -> none  [the longest x1 50.4 us: per_device(): lax.psum(grad_normed_part, 'tp')]
    all_gather x4 -> x0, blocking collectives: 75.4 us -> none  [the longest x1 26.9 us: fetch_dense(): lax.all_gather(router, 'ctx', axis=0, tiled=True)]
    gather x6 -> x0, local copies, waits for them, and re-layouts: 41 us -> none  [the longest x2 14.2 us: per_device(): expert_in = normed_ffn[source_rows].reshape(expert_count, -1, model_width)]
  transfers between devices with their start and end apart: 27 -> 0, of which waited for: 23 -> 0; matrix products, arithmetic and copies ran while one was open for 13% -> 0% of each run, Pallas kernels for 0% -> 0%
where the time goes in v2:
time: 553 us; the launch traced here: 543 us
  Pallas kernels  512 us (93%)
  local copies, waits for them, and re-layouts  19.4 us (4%)
  other arithmetic  10.2 us (2%)
    pallas_call x1, Pallas kernels, later(): pl.pallas_call(later_kernel, out_shape=(tokens, tokens, expert, expert, e...  347 us
    pallas_call x1, Pallas kernels, forward(): pl.pallas_call(forward_kernel, out_shape=(jax.ShapeDtypeStruct((2, 32, wi...  166 us

profile of v2, /device:TPU:29, one launch (start us, length us, event | category | flops | bytes accessed | tf_op | source)
XLA Modules:
  0.0 543.4 jit_solution(15340490746899733531)
XLA Ops:
  1.5 0.7 broadcast_in_dim.6
  2.2 0.7 broadcast_in_dim.14
  2.8 0.8 fusion.2
  3.7 0.8 concatenate.3
  5.1 165.8 %shard_map.255 = (bf16[2,32,2048]{2,1,0:T(8,128)(2,1)}, bf16[4,2,8,32,2048]{4,3,2,1,0:T(8,128)(2,1)}, bf16[2,2048,256]{2,1,0:T(8,128)(2,1)}, bf16[2,2048,256]{2,...) custom-call(bf16[4,64,2048]{2,1,0:T(8,128)(2,1)} %tokens.1, ...), custom_call_target="tpu_custom_call" | custom-call | flops 4000000000 | bytes 64000000 | tf_op jit(solution)/shard_map/pallas_call | solution.py:912
  170.9 0.9 slice.31
  172.6 0.9 pad.9.chosen
  173.5 346.6 %shard_map.256 = (bf16[4,64,2048]{2,1,0:T(8,128)(2,1)}, bf16[4,64,2048]{2,1,0:T(8,128)(2,1)}, bf16[16,256,256]{2,1,0:T(8,128)(2,1)}, bf16[16,256,256]{2,1,0:T(8,...) custom-call(bf16[2,32,2048]{2,1,0:T(8,128)(2,1)} %get-tuple-element., ...), custom_call_target="tpu_custom_call" | custom-call | flops 48000000000 | bytes 64000000 | tf_op jit(solution)/shard_map/pallas_call | solution.py:1531
  520.2 0.7 slice.34
  520.9 0.6 dynamic-slice_bitcast_fusion
  521.5 1.3 fusion.5
  522.8 1.3 slice_bitcast_fusion
  524.2 1.4 convert_bitcast_fusion
  525.6 1.1 fusion.4
  526.7 2.2 copy.44
  528.9 2.0 copy.43
  531.0 1.0 copy.42
  531.9 1.0 copy.41
  532.9 2.5 convert_element_type.29
  535.4 2.5 convert_element_type.30
  537.9 2.5 convert_element_type.31
  540.3 1.0 copy.47
  541.3 0.6 copy-done.5
  542.0 1.0 copy.48
  (21 shorter events, 2.4 us)
Async XLA Ops:
  0.6 0.7 copy-start
  526.7 6.2 %copy-start.4 = (bf16[16,256,256]{2,1,0:T(8,128)(2,1)S(1)}, bf16[16,256,256]{2,1,0:T(8,128)(2,1)}, u32[]{:S(2)}) copy-start(bf16[16,256,256]{2,1,0:T(8,128)(2,1)} %get-tuple-element.54) | copy-start | bytes 6291460
  532.9 2.5 copy-start.3
  535.4 2.5 copy-start.2
  537.9 2.5 copy-start.6
  537.9 5.0 copy-start.1
  540.3 1.6 copy-start.5
